TPU v7x, 128 devices: a whole 4x4x4 slice. The times are simulated.
128 devices in a mesh: expert: 32 (over y, x, core), tensor: 4 (over z).
Axes of the slice: x: 4, y: 4, z: 4, core: 2. Of those that a mesh axis runs over, the one named last changes fastest.
Arguments:
- block_input: bfloat16 [4096, 2880], P('expert'), may hold values from -6 to 6
- out_cotangent: bfloat16 [4096, 2880], P('expert'), may hold values from -6 to 6
- seq_lengths: int32 [32, 4], P('expert'), may hold values from 1 to 64, 128 in all within a row
- route_ids: int32 [4096, 4], P('expert'), may hold values from 0 to 31, all different within a row; in each aligned block of 128 rows (0 to 127, 128 to 255, ...) at most 32 rows name the same one
- attn_gain: float32 [2880], replicated, may hold values from 0.5 to 1.5
- w_query: bfloat16 [2880, 4096], P('expert', 'tensor'), may hold values from -0.109375 to 0.109375
- w_key: bfloat16 [2880, 512], P('expert', 'tensor'), may hold values from -0.109375 to 0.109375
- w_value: bfloat16 [2880, 512], P('expert', 'tensor'), may hold values from -0.109375 to 0.109375
- b_query: float32 [4096], P('tensor'), may hold values from -1.2 to 1.2
- b_key: float32 [512], P('tensor'), may hold values from -1.2 to 1.2
- b_value: float32 [512], P('tensor'), may hold values from -1.2 to 1.2
- sink_logits: float32 [64], P('tensor'), may hold values from -4 to 4
- w_output: bfloat16 [4096, 2880], P('tensor', 'expert'), may hold values from -0.25 to 0.25
- b_output: float32 [2880], replicated, may hold values from -1.2 to 1.2
- ffn_gain: float32 [2880], replicated, may hold values from 0.5 to 1.5
- w_router: float32 [2880, 32], replicated, may hold values from -0.0546875 to 0.0546875
- b_router: float32 [32], replicated, may hold values from -3 to 3
- w_gate: bfloat16 [32, 2880, 2880], P('expert', None, 'tensor'), may hold values from -0.109375 to 0.109375
- w_up: bfloat16 [32, 2880, 2880], P('expert', None, 'tensor'), may hold values from -0.109375 to 0.109375
- b_gate: float32 [32, 2880], P('expert', 'tensor'), may hold values from -0.6 to 0.6
- b_up: float32 [32, 2880], P('expert', 'tensor'), may hold values from -0.6 to 0.6
- w_down: bfloat16 [32, 2880, 2880], P('expert', 'tensor'), may hold values from -0.109375 to 0.109375
- b_down: float32 [32, 2880], P('expert'), may hold values from -0.6 to 0.6
Outputs:
- block_output: bfloat16 [4096, 2880], P('expert')
- input_grad: float32 [4096, 2880], P('expert')
- attn_gain_grad: float32 [2880], replicated
- w_query_grad: float32 [2880, 4096], P('expert', 'tensor')
- w_key_grad: float32 [2880, 512], P('expert', 'tensor')
- w_value_grad: float32 [2880, 512], P('expert', 'tensor')
- b_query_grad: float32 [4096], P('tensor')
- b_key_grad: float32 [512], P('tensor')
- b_value_grad: float32 [512], P('tensor')
- sink_grad: float32 [64], P('tensor')
- w_output_grad: float32 [4096, 2880], P('tensor', 'expert')
- b_output_grad: float32 [2880], replicated
- ffn_gain_grad: float32 [2880], replicated
- w_router_grad: float32 [2880, 32], replicated
- b_router_grad: float32 [32], replicated
- w_gate_grad: float32 [32, 2880, 2880], P('expert', None, 'tensor')
- w_up_grad: float32 [32, 2880, 2880], P('expert', None, 'tensor')
- b_gate_grad: float32 [32, 2880], P('expert', 'tensor')
- b_up_grad: float32 [32, 2880], P('expert', 'tensor')
- w_down_grad: float32 [32, 2880, 2880], P('expert', 'tensor')
- b_down_grad: float32 [32, 2880], P('expert')
Inputs may be any that keep to these rules, and one draw needn't show every extreme that they name: `seq_lengths`: each row lists in order the lengths of the 4 sequences packed into one device's 128 tokens; they sum to 128 and the longest is exactly 64. `route_ids`: each row names 4 different experts; within the rows of one device no expert is named more than 32 times, and in some device's rows an expert is named exactly 32 times.
All inputs are finite; a program needn't handle non-finite values.
Results may differ from a plain program's by a relative error of at most 0.034.
Values may be sent and summed in bfloat16 or wider, within the bound.
No kernel may reach another device: no remote copies, remote signals or barrier semaphores. Data moves between devices by JAX's collectives and lax.ppermute only.
A program may use at most 256 MiB of HBM per device.

v0:
```python
import functools

import jax
import jax.numpy as jnp
from jax import lax
from jax.experimental import pallas as pl
from jax.experimental.pallas import tpu as pltpu
from jax.sharding import PartitionSpec as P

HD = 64
PAIR = 2 * HD
EPSILON = 1e-05
ROPE_BASE = 150000.0
CLAMP_LIMIT = 7.0
GLU_SLOPE = 1.702
MASKED = -1e30
PRECISE = lax.Precision.HIGHEST
LOW = jnp.bfloat16
F32 = jnp.float32
VMEM_BYTES = 56 * 1024 * 1024
NN = (((1,), (0,)), ((), ()))
NT = (((1,), (1,)), ((), ()))
TN = (((0,), (0,)), ((), ()))


def round_up(value, unit):
    return -(-value // unit) * unit


def dot(left, right, dims=NN):
    return lax.dot_general(left, right, dims, preferred_element_type=F32)


def split_low(values):
    high = values.astype(LOW)
    return high, (values - high.astype(F32)).astype(LOW)


def layout(lengths, tok_count):
    seq_ends = jnp.cumsum(lengths)
    tok_index = jnp.arange(tok_count, dtype=jnp.int32)
    is_past = tok_index[:, None] >= seq_ends[None, :]
    segment = jnp.sum(is_past.astype(jnp.int32), axis=1)
    offset = jnp.sum(jnp.where(is_past, lengths[None, :], 0), axis=1)
    return (segment, tok_index - offset)


def rope_tables(position):
    half = HD // 2
    frequency = ROPE_BASE ** (-(jnp.arange(half).astype(F32) * 2.0 / HD))
    angles = position.astype(F32)[:, None] * frequency[None, :]
    cosine, sine = jnp.cos(angles), jnp.sin(angles)
    return (
        jnp.concatenate([cosine] * 4, axis=1),
        jnp.concatenate([-sine, sine, -sine, sine], axis=1),
    )


def lane_index(shape):
    return lax.broadcasted_iota(jnp.int32, shape, len(shape) - 1)


def swap_halves(values):
    first = (lane_index(values.shape) % HD) < HD // 2
    return jnp.where(
        first, pltpu.roll(values, PAIR - HD // 2, 1), pltpu.roll(values, HD // 2, 1)
    )


def twin(values, which):
    turned = pltpu.roll(values, HD, 1)
    left = lane_index(values.shape) < HD
    return jnp.where(left, values, turned) if which == 0 else jnp.where(left, turned, values)


def attend_forward_kernel(
    sink_ref,
    rows_ref,
    weights_ref,
    bias_ref,
    cos_ref,
    sin_ref,
    allowed_ref,
    out_ref,
    rot_ref,
    lse_ref,
    qkv_ref,
):
    step = pl.program_id(0)
    start = weights_ref.shape[1] - qkv_ref.shape[1]
    part = dot(rows_ref[...], weights_ref[:, start:])

    @pl.when(step == 0)
    def _():
        qkv_ref[...] = part + bias_ref[...]

    @pl.when(step > 0)
    def _():
        qkv_ref[...] += part

    @pl.when(step == pl.num_programs(0) - 1)
    def _():
        attend(
            sink_ref, qkv_ref, cos_ref, sin_ref, allowed_ref, out_ref, rot_ref, lse_ref
        )


def attend(sink_ref, qkv_ref, cos_ref, sin_ref, allowed_ref, out_ref, rot_ref, lse_ref):
    tokens = qkv_ref.shape[0]
    heads = sink_ref.shape[0]
    key_at = heads * HD
    value_at = key_at + PAIR
    per_group = heads // 2
    cos, sin = cos_ref[...], sin_ref[...]
    allowed = allowed_ref[...] > 0.5
    left = lane_index((tokens, PAIR)) < HD
    lanes = lane_index((tokens, PAIR))

    def rope(values):
        return values * cos + swap_halves(values) * sin

    key = rope(qkv_ref[:, key_at:value_at])
    value = qkv_ref[:, value_at : value_at + PAIR]
    rot_ref[:, key_at:value_at] = key.astype(LOW)
    rot_ref[:, value_at : value_at + PAIR] = value.astype(LOW)
    keys = [twin(key, g).astype(LOW) for g in range(2)]
    values = [twin(value, g).astype(LOW) for g in range(2)]
    lse_all = jnp.zeros((tokens, PAIR), F32)
    for pair in range(heads // 2):
        cols = slice(pair * PAIR, (pair + 1) * PAIR)
        group = (2 * pair) // per_group
        query = rope(qkv_ref[:, cols])
        rot_ref[:, cols] = query.astype(LOW)
        outs = []
        for side in range(2):
            head = 2 * pair + side
            mine = left if side == 0 else jnp.logical_not(left)
            one = jnp.where(mine, query, 0.0).astype(LOW)
            scores = dot(one, keys[group], NT) * HD ** (-0.5)
            scores = jnp.where(allowed, scores, MASKED)
            sink = sink_ref[head]
            top = jnp.maximum(jnp.max(scores, axis=1, keepdims=True), sink)
            weights = jnp.exp(scores - top)
            denom = jnp.sum(weights, axis=1, keepdims=True) + jnp.exp(sink - top)
            lse = top + jnp.log(denom)
            lse_all = jnp.where(lanes == head, lse, lse_all)
            prob = (weights / denom).astype(LOW)
            outs.append(dot(prob, values[group]))
        out_ref[:, cols] = jnp.where(left, outs[0], outs[1]).astype(LOW)
    lse_ref[...] = lse_all


def attend_backward_kernel(
    sink_ref,
    rows_ref,
    weights_ref,
    rot_ref,
    lse_ref,
    cos_ref,
    sin_ref,
    allowed_ref,
    out_ref,
    sink_out_ref,
    sum_ref,
    grad_ref,
):
    step = pl.program_id(0)
    part = dot(rows_ref[...], weights_ref[...])

    @pl.when(step == 0)
    def _():
        sum_ref[...] = part

    @pl.when(step > 0)
    def _():
        sum_ref[...] += part

    @pl.when(step == pl.num_programs(0) - 1)
    def _():
        grad_ref[...] = sum_ref[...].astype(LOW)
        attend_back(
            sink_ref,
            rot_ref,
            grad_ref,
            lse_ref,
            cos_ref,
            sin_ref,
            allowed_ref,
            out_ref,
            sink_out_ref,
        )


def attend_back(
    sink_ref, rot_ref, grad_ref, lse_ref, cos_ref, sin_ref, allowed_ref, out_ref, sink_out_ref
):
    tokens = rot_ref.shape[0]
    heads = sink_ref.shape[0]
    key_at = heads * HD
    value_at = key_at + PAIR
    per_group = heads // 2
    scale = HD ** (-0.5)
    cos, sin = cos_ref[...], sin_ref[...]
    allowed = allowed_ref[...] > 0.5
    lanes = lane_index((tokens, PAIR))
    left = lanes < HD

    def turn_back(values):
        return values * cos - swap_halves(values) * sin

    key = rot_ref[:, key_at:value_at].astype(F32)
    value = rot_ref[:, value_at : value_at + PAIR].astype(F32)
    keys = [twin(key, g).astype(LOW) for g in range(2)]
    values = [twin(value, g).astype(LOW) for g in range(2)]
    key_sums = [jnp.zeros((tokens, PAIR), F32) for _ in range(2)]
    value_sums = [jnp.zeros((tokens, PAIR), F32) for _ in range(2)]
    sink_all = jnp.zeros((tokens, PAIR), F32)
    lse_all = lse_ref[...]
    for pair in range(heads // 2):
        cols = slice(pair * PAIR, (pair + 1) * PAIR)
        group = (2 * pair) // per_group
        query = rot_ref[:, cols].astype(F32)
        grad = grad_ref[:, cols].astype(F32)
        outs = []
        for side in range(2):
            head = 2 * pair + side
            mine = left if side == 0 else jnp.logical_not(left)
            one = jnp.where(mine, query, 0.0).astype(LOW)
            grad_one = jnp.where(mine, grad, 0.0).astype(LOW)
            lse = jnp.sum(jnp.where(lanes == head, lse_all, 0.0), axis=1, keepdims=True)
            scores = dot(one, keys[group], NT) * scale
            prob = jnp.where(allowed, jnp.exp(jnp.where(allowed, scores - lse, 0.0)), 0.0)
            grad_prob = dot(grad_one, values[group], NT)
            delta = jnp.sum(prob * grad_prob, axis=1, keepdims=True)
            grad_score = (prob * (grad_prob - delta)).astype(LOW)
            outs.append(dot(grad_score, keys[group]))
            key_sums[group] += dot(grad_score, one, TN)
            value_sums[group] += dot(prob.astype(LOW), grad_one, TN)
            sink_all = jnp.where(lanes == head, jnp.exp(sink_ref[head] - lse) * delta, sink_all)
        out_ref[:tokens, cols] = turn_back(jnp.where(left, outs[0], outs[1]) * scale).astype(LOW)

    def fold(sums):
        both = [one + pltpu.roll(one, HD, 1) for one in sums]
        return jnp.where(left, both[0], both[1])

    out_ref[:tokens, key_at:value_at] = turn_back(fold(key_sums) * scale).astype(LOW)
    out_ref[:tokens, value_at : value_at + PAIR] = fold(value_sums).astype(LOW)
    sink_out_ref[...] = -jnp.sum(sink_all, axis=0, keepdims=True)


def kernel_params():
    return pltpu.CompilerParams(vmem_limit_bytes=VMEM_BYTES)


SHORT = pl.CostEstimate(flops=1, bytes_accessed=1, transcendentals=0)
IN_VMEM = pl.BlockSpec(memory_space=pltpu.VMEM)
IN_SMEM = pl.BlockSpec(memory_space=pltpu.SMEM)


def by_row(block, columns):
    return pl.BlockSpec((block, columns), lambda i: (i, 0))


def by_column(rows, block):
    return pl.BlockSpec((rows, block), lambda i: (0, i))


def whole_block(*shape):
    return pl.BlockSpec(shape, lambda i: (0, 0))


def held_block(*shape):
    return pl.BlockSpec(shape, lambda i: (0, 0), pipeline_mode=pl.Buffered(1))


STEPS = 4


def attend_forward(sinks, rows, weights, bias, cos, sin, allowed):
    tokens, inner = rows.shape
    width = bias.shape[1]
    heads = sinks.shape[0]
    block = inner // STEPS
    return pl.pallas_call(
        attend_forward_kernel,
        grid=(STEPS,),
        out_shape=(
            jax.ShapeDtypeStruct((tokens, heads * HD), LOW),
            jax.ShapeDtypeStruct((tokens, width), LOW),
            jax.ShapeDtypeStruct((tokens, PAIR), F32),
        ),
        in_specs=[
            IN_SMEM,
            by_column(tokens, block),
            by_row(block, weights.shape[1]),
            whole_block(1, width),
            whole_block(*cos.shape),
            whole_block(*sin.shape),
            whole_block(*allowed.shape),
        ],
        out_specs=(
            whole_block(tokens, heads * HD),
            whole_block(tokens, width),
            whole_block(tokens, PAIR),
        ),
        scratch_shapes=[pltpu.VMEM((tokens, width), F32)],
        compiler_params=kernel_params(),
        cost_estimate=SHORT,
        name="attend_forward",
    )(sinks, rows, weights, bias, cos, sin, allowed)


def attend_backward(sinks, rows, weights, rotated, lse, cos, sin, allowed):
    tokens, width = rotated.shape
    inner = rows.shape[1]
    out_width = sinks.shape[0] * HD
    block = inner // STEPS
    return pl.pallas_call(
        attend_backward_kernel,
        grid=(STEPS,),
        out_shape=(
            jax.ShapeDtypeStruct((tokens, width), LOW),
            jax.ShapeDtypeStruct((1, PAIR), F32),
        ),
        in_specs=[
            IN_SMEM,
            by_column(tokens, block),
            by_row(block, out_width),
            whole_block(tokens, width),
            whole_block(*lse.shape),
            whole_block(*cos.shape),
            whole_block(*sin.shape),
            whole_block(*allowed.shape),
        ],
        out_specs=(whole_block(tokens, width), whole_block(1, PAIR)),
        scratch_shapes=[pltpu.VMEM((tokens, out_width), F32), pltpu.VMEM((tokens, out_width), LOW)],
        compiler_params=kernel_params(),
        cost_estimate=SHORT,
        name="attend_backward",
    )(sinks, rows, weights, rotated, lse, cos, sin, allowed)


def compact_kernel(shard, shard_pad, left_ref, weights_ref, *refs):
    unit_ref, upper_ref, lower_ref, gain_ref = refs if len(refs) == 4 else (None, *refs, None)
    start = weights_ref.shape[1] - left_ref.shape[1]
    product = dot(left_ref[...], weights_ref[:, start:], NT)
    half = upper_ref.shape[0]
    shards = weights_ref.shape[0] // shard_pad
    if gain_ref is not None:
        gain = jnp.sum(product * unit_ref[...].astype(F32), axis=0, keepdims=True)
    for step in range(upper_ref.shape[1] // (shards * shard)):

        @pl.when(pl.program_id(0) == step)
        def _():
            for i in range(shards):
                piece = product[:, i * shard_pad : i * shard_pad + shard].astype(LOW)
                at = (step * shards + i) * shard
                upper_ref[:, at : at + shard] = piece[:half]
                lower_ref[:, at : at + shard] = piece[half:]
                if gain_ref is not None:
                    pad_at = i * shard_pad
                    gain_ref[:, at : at + shard] = gain[:, pad_at : pad_at + shard]


def compact_product(left, tokens, weights, block_width, shard, shard_pad, name, unit=None):
    inner = left.shape[1]
    rows = weights.shape[0]
    features = rows // shard_pad * shard
    half = jax.ShapeDtypeStruct((tokens // 2, features), LOW)
    operands = [left, weights]
    in_specs = [whole_block(tokens, inner), by_row(rows // STEPS, block_width)]
    out_shape = [half, half]
    if unit is not None:
        operands.append(unit)
        in_specs.append(by_column(tokens, rows // STEPS))
        out_shape.append(jax.ShapeDtypeStruct((1, features), F32))
    return pl.pallas_call(
        functools.partial(compact_kernel, shard, shard_pad),
        grid=(STEPS,),
        out_shape=out_shape,
        in_specs=in_specs,
        out_specs=[whole_block(*one.shape) for one in out_shape],
        compiler_params=kernel_params(),
        cost_estimate=SHORT,
        name=name,
    )(*operands)


def rms_scale(values):
    return lax.rsqrt(jnp.mean(values * values, axis=1, keepdims=True) + EPSILON)


def join_halves(halves, out_ref):
    upper, upper_in, lower, lower_in = halves
    half = upper.shape[0]
    out_ref[:half, :] = upper[...].astype(F32) + upper_in[...].astype(F32)
    out_ref[half:, :] = lower[...].astype(F32) + lower_in[...].astype(F32)


def token_forward_kernel(place_ref, input_ref, *refs):
    halves, refs = refs[:4], refs[4:]
    bias_ref, gain_ref, router_ref, router_bias_ref, named_ref, slots_ref = refs[:6]
    resid_ref, gates_ref, sent_ref, own_ref = refs[6:]
    features = input_ref.shape[1]
    experts = router_ref.shape[0]
    chunk = own_ref.shape[1]
    join_halves(halves, resid_ref)
    resid = input_ref[...].astype(F32) + resid_ref[...] + bias_ref[...]
    resid_ref[...] = resid
    normed = resid * rms_scale(resid) * gain_ref[...]
    logits = lax.dot_general(
        normed, router_ref[...], NT, precision=PRECISE, preferred_element_type=F32
    )
    named = named_ref[...] > 0.5
    logits = jnp.where(named, logits + router_bias_ref[...], MASKED)
    weights = jnp.exp(logits - jnp.max(logits, axis=1, keepdims=True))
    weights = jnp.where(named, weights, 0.0)
    gates = weights / jnp.sum(weights, axis=1, keepdims=True)
    gates_ref[...] = gates
    high, low = split_low(gates)
    sent_ref[:, :features] = normed.astype(LOW)
    sent_ref[:, features : features + experts] = high
    sent_ref[:, features + experts : features + 2 * experts] = low
    spare = sent_ref.shape[1] - features - 2 * experts
    if spare:
        sent_ref[:, features + 2 * experts :] = jnp.zeros((resid.shape[0], spare), LOW)
    own = sent_ref[:, pl.ds(pl.multiple_of(place_ref[0] * chunk, 128), chunk)]
    own_ref[...] = dot(slots_ref[...], own).astype(LOW)


def token_forward(place, inputs, halves, bias, gain, router, router_bias, named, slots, width, chunk):
    tokens, features = inputs.shape
    experts = router.shape[0]
    return pl.pallas_call(
        token_forward_kernel,
        out_shape=(
            jax.ShapeDtypeStruct((tokens, features), F32),
            jax.ShapeDtypeStruct((tokens, experts), F32),
            jax.ShapeDtypeStruct((tokens, width), LOW),
            jax.ShapeDtypeStruct((slots.shape[0], chunk), LOW),
        ),
        in_specs=[IN_SMEM] + [IN_VMEM] * 11,
        out_specs=(IN_VMEM,) * 4,
        compiler_params=kernel_params(),
        cost_estimate=SHORT,
        name="token_forward",
    )(place, inputs, *halves, bias, gain, router, router_bias, named, slots)


def token_backward_kernel(shard, shard_pad, place_ref, *refs):
    near_halves, halves, refs = refs[:4], refs[4:8], refs[8:]
    gates_ref, router_ref, resid_ref, cotangent_ref, gain_ref = refs[:5]
    out_ref, spread_ref, blocks_ref, router_out_ref, vectors_ref = refs[5:10]
    near_ref, far_ref, grad_ref, router_all_ref = refs[10:]
    tokens, features = resid_ref.shape
    experts = router_ref.shape[0]
    split = near_ref.shape[1]
    rest = features - split
    join_halves(near_halves, near_ref)
    join_halves(halves, far_ref)
    gates = gates_ref[...]
    grad_gates = far_ref[:, rest : rest + experts] + far_ref[:, rest + experts : rest + 2 * experts]
    grad_logits = gates * (grad_gates - jnp.sum(gates * grad_gates, axis=1, keepdims=True))
    through = lax.dot_general(
        grad_logits, router_ref[...], NN, precision=PRECISE, preferred_element_type=F32
    )
    grad_ref[:, :split] = through[:, :split] + near_ref[...]
    grad_ref[:, split:] = through[:, split:] + far_ref[:, :rest]
    grad_two = grad_ref[...]
    resid = resid_ref[...]
    scale = rms_scale(resid)
    unit = resid * scale
    gain = gain_ref[...]
    router_part = lax.dot_general(
        grad_logits, unit * gain, TN, precision=PRECISE, preferred_element_type=F32
    )
    scaled = grad_two * gain
    mean = jnp.mean(unit * scaled, axis=1, keepdims=True)
    grad_resid = cotangent_ref[...].astype(F32) + scale * (scaled - unit * mean)
    out_ref[...] = grad_resid
    vectors_ref[...] = jnp.zeros_like(vectors_ref)
    vectors_ref[0:1, :features] = jnp.sum(grad_two * unit, axis=0, keepdims=True)
    vectors_ref[1:2, :features] = jnp.sum(grad_resid, axis=0, keepdims=True)
    vectors_ref[2:3, :experts] = jnp.sum(grad_logits, axis=0, keepdims=True)
    low = grad_resid.astype(LOW)
    for i in range(features // shard):
        at = i * shard_pad
        spread_ref[:, at : at + shard] = low[:, i * shard : (i + 1) * shard]
        spread_ref[:, at + shard : at + shard_pad] = jnp.zeros((tokens, shard_pad - shard), LOW)
    turned = spread_ref[...].T
    for i in range(features // shard):
        blocks_ref[i] = turned[i * shard_pad : (i + 1) * shard_pad]
    router_all_ref[:, :features] = router_part.astype(LOW)
    spare = router_all_ref.shape[1] - features
    router_all_ref[:, features:] = jnp.zeros((router_part.shape[0], spare), LOW)
    block = router_out_ref.shape[1]
    start = pl.multiple_of(place_ref[0] * block, 128)
    router_out_ref[...] = router_all_ref[:, pl.ds(start, block)]


def pack_kernel(router_ref, vectors_ref, gain_ref, sinks_ref, out_ref):
    experts, width = router_ref.shape
    features = gain_ref.shape[1]
    out_ref[...] = jnp.zeros_like(out_ref)
    out_ref[:experts, :] = router_ref[...]
    row = experts
    for values in (gain_ref[...], vectors_ref[0:1, :features], vectors_ref[1:2, :features]):
        for at in range(0, features, width):
            piece = values[:, at : at + width].astype(LOW)
            out_ref[row : row + 1, : piece.shape[1]] = piece
            row += 1
    lanes = sinks_ref.shape[1]
    out_ref[row : row + 1, :lanes] = sinks_ref[...].astype(LOW)
    out_ref[row + 1 : row + 2, :lanes] = vectors_ref[2:3, :lanes].astype(LOW)


def pack_small(router, vectors, gain, sinks):
    experts, width = router.shape
    rows = round_up(experts + 3 * -(-gain.shape[1] // width) + 2, 16)
    return pl.pallas_call(
        pack_kernel,
        out_shape=jax.ShapeDtypeStruct((rows, width), LOW),
        in_specs=[IN_VMEM] * 4,
        out_specs=IN_VMEM,
        compiler_params=kernel_params(),
        cost_estimate=SHORT,
        name="pack_small",
    )(router, vectors, gain, sinks)


def unpack_kernel(place_ref, *refs):
    chunk_refs, (scale_ref, rest_ref), refs = refs[:4], refs[4:6], refs[6:]
    router_ref, gain_ref, first_ref, second_ref, sinks_ref, bias_ref, all_ref, vector_ref = refs
    experts, features = router_ref.shape
    width = chunk_refs[0].shape[1]
    assemble(place_ref, chunk_refs, all_ref)
    router_ref[...] = all_ref[:experts, :features].astype(F32)
    tiles = -(-features // width)
    for tile in range(tiles):
        at = tile * width
        size = min(width, features - at)
        row = experts + tile
        parts = all_ref[row : row + 1, :].astype(F32)
        total = sum(parts[:, i * width : (i + 1) * width] for i in range(4))
        vector_ref[0:1, at : at + size] = total[:, :size]
        for i in range(2):
            row = i * tiles + tile
            vector_ref[i + 1 : i + 2, at : at + size] = rest_ref[row : row + 1, :size].astype(F32)
    gain_ref[...] = (vector_ref[0:1, :] / scale_ref[...]).reshape(features)
    first_ref[...] = vector_ref[1:2, :].reshape(features)
    second_ref[...] = vector_ref[2:3, :].reshape(features)
    row = 2 * tiles
    heads, biases = sinks_ref.shape[0], bias_ref.shape[0]
    sinks_ref[...] = rest_ref[row : row + 1, :heads].astype(F32).reshape(heads)
    bias_ref[...] = rest_ref[row + 1 : row + 2, :biases].astype(F32).reshape(biases)


def unpack_small(place, chunks, rest, gain, experts, heads):
    rows, width = chunks[0].shape
    features = gain.shape[1]
    wide = jax.ShapeDtypeStruct((features,), F32)
    return pl.pallas_call(
        unpack_kernel,
        out_shape=(
            jax.ShapeDtypeStruct((experts, features), F32),
            wide,
            wide,
            wide,
            jax.ShapeDtypeStruct((heads,), F32),
            jax.ShapeDtypeStruct((experts,), F32),
        ),
        in_specs=[IN_SMEM] + [IN_VMEM] * 6,
        out_specs=(IN_VMEM,) * 6,
        scratch_shapes=[
            pltpu.VMEM((rows, len(chunks) * width), LOW),
            pltpu.VMEM((8, features), F32),
        ],
        compiler_params=kernel_params(),
        cost_estimate=SHORT,
        name="unpack_small",
    )(place, *chunks, gain, rest)


def gathered_kernel(shard, blocks_ref, rows_ref, *refs):
    *out_refs, sum_ref = refs
    blocks = blocks_ref.shape[0]
    tokens = blocks_ref.shape[2]
    total = None
    for i in range(blocks):
        rows = rows_ref[i * tokens : (i + 1) * tokens, :]
        part = dot(blocks_ref[i], rows)
        total = part if total is None else total + part
    first = pl.program_id(0) == 0

    @pl.when(first)
    def _():
        sum_ref[...] = total

    @pl.when(jnp.logical_not(first))
    def _():
        sum_ref[...] += total

    @pl.when(pl.program_id(0) == pl.num_programs(0) - 1)
    def _():
        at = 0
        for out_ref in out_refs[: len(out_refs) // 2 if len(out_refs) > 1 else 1]:
            out_ref[...] = sum_ref[:shard, at : at + out_ref.shape[1]]
            at += out_ref.shape[1]
        at = 0
        for out_ref in out_refs[len(out_refs) // 2 if len(out_refs) > 1 else 1 :]:
            size = out_ref.shape[0]
            out_ref[...] = sum_ref[shard : shard + 1, at : at + size].reshape(size)
            at += size


def gathered_products(blocks, which, rows, widths, shard, shard_pad, biases, name):
    parts, _, tokens = blocks.shape
    total, width = rows.shape
    block = parts // STEPS
    out_shape = [jax.ShapeDtypeStruct((shard, one), F32) for one in widths]
    if biases:
        out_shape += [jax.ShapeDtypeStruct((one,), F32) for one in widths]
    return pl.pallas_call(
        functools.partial(gathered_kernel, shard),
        grid=(STEPS,),
        out_shape=out_shape,
        in_specs=[
            pl.BlockSpec((block, shard_pad, tokens), lambda i: (i, which, 0)),
            by_row(total // STEPS, width),
        ],
        out_specs=[
            pl.BlockSpec(one.shape, lambda i, rank=len(one.shape): (0,) * rank)
            for one in out_shape
        ],
        scratch_shapes=[pltpu.VMEM((shard_pad, width), F32)],
        compiler_params=kernel_params(),
        cost_estimate=SHORT,
        name=name,
    )(blocks, rows)


def token_backward(
    place, near, halves, gates, router, resid, cotangent, gain, shard, shard_pad, ring
):
    tokens, features = resid.shape
    experts = router.shape[0]
    router_block = round_up(-(-features // ring), 128)
    parts = features // shard
    return pl.pallas_call(
        functools.partial(token_backward_kernel, shard, shard_pad),
        out_shape=(
            jax.ShapeDtypeStruct((tokens, features), F32),
            jax.ShapeDtypeStruct((tokens, features // shard * shard_pad), LOW),
            jax.ShapeDtypeStruct((parts, shard_pad, tokens), LOW),
            jax.ShapeDtypeStruct((experts, router_block), LOW),
            jax.ShapeDtypeStruct((8, router_block * ring), F32),
        ),
        in_specs=[IN_SMEM] + [IN_VMEM] * 13,
        out_specs=(IN_VMEM,) * 5,
        scratch_shapes=[
            pltpu.VMEM((tokens, near[0].shape[1]), F32),
            pltpu.VMEM((tokens, halves[0].shape[1]), F32),
            pltpu.VMEM((tokens, features), F32),
            pltpu.VMEM((experts, router_block * ring), LOW),
        ],
        compiler_params=kernel_params(),
        cost_estimate=SHORT,
        name="token_backward",
    )(place, *near, *halves, gates, router, resid, cotangent, gain)


def output_kernel(place_ref, *refs):
    near_refs, (resid_ref, out_ref, near_ref) = refs[:4], refs[4:]
    assemble(place_ref, near_refs, near_ref)
    near = near_ref[:, : out_ref.shape[0]].astype(F32)
    out_ref[...] = (resid_ref[...] + near).astype(LOW).T


def output_rows(place, near, resid):
    tokens, features = resid.shape
    return pl.pallas_call(
        output_kernel,
        out_shape=jax.ShapeDtypeStruct((features, tokens), LOW),
        in_specs=[IN_SMEM] + [IN_VMEM] * 5,
        out_specs=IN_VMEM,
        scratch_shapes=[pltpu.VMEM((tokens, sum(one.shape[1] for one in near)), LOW)],
        compiler_params=kernel_params(),
        cost_estimate=SHORT,
        name="output_rows",
    )(place, *near, resid)


def mix_kernel(place_ref, gates_ref, rows_ref, out_ref):
    experts, slots = gates_ref.shape[1], place_ref.shape[1]
    own = lax.broadcasted_iota(jnp.int32, (experts, slots), 1) // (slots // experts)
    own = own == lax.broadcasted_iota(jnp.int32, (experts, slots), 0)
    spread = dot(gates_ref[...].astype(LOW), own.astype(F32).astype(LOW))
    weights = (place_ref[...].astype(F32) * spread).astype(LOW)
    out_ref[...] = dot(weights, rows_ref[...]).astype(LOW)


def mix_results(place_t, gates, rows):
    return pl.pallas_call(
        mix_kernel,
        out_shape=jax.ShapeDtypeStruct((place_t.shape[0], rows.shape[1]), LOW),
        in_specs=[IN_VMEM] * 3,
        out_specs=IN_VMEM,
        compiler_params=kernel_params(),
        cost_estimate=SHORT,
        name="mix_results",
    )(place_t, gates, rows)


def input_grad_kernel(*refs):
    halves, (resid_ref, input_ref, gain_ref, out_ref, sum_ref) = refs[:4], refs[4:]
    join_halves(halves, sum_ref)
    inputs = input_ref[...].astype(F32)
    scale = rms_scale(inputs)
    unit = inputs * scale
    scaled = sum_ref[...] * gain_ref[...]
    mean = jnp.mean(unit * scaled, axis=1, keepdims=True)
    out_ref[...] = (resid_ref[...] + scale * (scaled - unit * mean)).T


def input_grad_rows(halves, resid, inputs, gain):
    tokens, features = resid.shape
    return pl.pallas_call(
        input_grad_kernel,
        out_shape=jax.ShapeDtypeStruct((features, tokens), F32),
        in_specs=[IN_VMEM] * 7,
        out_specs=IN_VMEM,
        scratch_shapes=[pltpu.VMEM((tokens, features), F32)],
        compiler_params=kernel_params(),
        cost_estimate=SHORT,
        name="input_grad",
    )(*halves, resid, inputs, gain)


def store_halves(values, rest, experts, upper_ref, lower_ref):
    half = upper_ref.shape[0]
    main = values[:, :rest].astype(LOW)
    upper_ref[:, :rest], lower_ref[:, :rest] = main[:half], main[half:]
    high, low = split_low(values[:, rest : rest + experts] + values[:, rest + experts : rest + 2 * experts])
    for out_ref, rows in ((upper_ref, slice(0, half)), (lower_ref, slice(half, 2 * half))):
        out_ref[:, rest : rest + experts] = high[rows]
        out_ref[:, rest + experts : rest + 2 * experts] = low[rows]
        spare = out_ref.shape[1] - rest - 2 * experts
        if spare:
            out_ref[:, rest + 2 * experts :] = jnp.zeros((half, spare), LOW)


def combine_kernel(rest, experts, place_ref, rows_ref, upper_ref, lower_ref):
    store_halves(dot(place_ref[...], rows_ref[...]), rest, experts, upper_ref, lower_ref)


def combine_far(place_t, rows, rest, experts):
    half = jax.ShapeDtypeStruct((place_t.shape[0] // 2, rows.shape[1]), LOW)
    return pl.pallas_call(
        functools.partial(combine_kernel, rest, experts),
        out_shape=(half, half),
        in_specs=[IN_VMEM] * 2,
        out_specs=(IN_VMEM,) * 2,
        compiler_params=kernel_params(),
        cost_estimate=SHORT,
        name="combine_far",
    )(place_t, rows)


def combine_near_kernel(place_ref, rows_ref, upper_ref, lower_ref):
    total = dot(place_ref[...], rows_ref[...]).astype(LOW)
    half = upper_ref.shape[0]
    upper_ref[...], lower_ref[...] = total[:half], total[half:]


def combine_near(place_t, rows):
    half = jax.ShapeDtypeStruct((place_t.shape[0] // 2, rows.shape[1]), LOW)
    return pl.pallas_call(
        combine_near_kernel,
        out_shape=(half, half),
        in_specs=[IN_VMEM] * 2,
        out_specs=(IN_VMEM,) * 2,
        compiler_params=kernel_params(),
        cost_estimate=SHORT,
        name="combine_near",
    )(place_t, rows)


def middle_kernel(rest, experts, *refs):
    halves, (upper_ref, lower_ref, sum_ref) = refs[:4], refs[4:]
    join_halves(halves, sum_ref)
    store_halves(sum_ref[...], rest, experts, upper_ref, lower_ref)


def middle_far(halves, rest, experts):
    half = jax.ShapeDtypeStruct(halves[0].shape, LOW)
    return pl.pallas_call(
        functools.partial(middle_kernel, rest, experts),
        out_shape=(half, half),
        in_specs=[IN_VMEM] * 4,
        out_specs=(IN_VMEM,) * 2,
        scratch_shapes=[pltpu.VMEM((2 * half.shape[0], half.shape[1]), F32)],
        compiler_params=kernel_params(),
        cost_estimate=SHORT,
        name="middle_far",
    )(*halves)


def assemble(place_ref, near_refs, out_ref):
    ring, width = len(near_refs), near_refs[0].shape[1]
    for ahead, near_ref in enumerate(near_refs):
        start = (place_ref[0] + ahead) % ring * width
        out_ref[:, pl.ds(pl.multiple_of(start, 128), width)] = near_ref[...]


def grad_hidden_kernel(place_ref, *refs):
    chunk_refs, (down_ref, bias_ref, out_ref, all_ref, rows_ref) = refs[:-5], refs[-5:]
    hidden, features = down_ref.shape
    assemble(place_ref, chunk_refs, rows_ref)
    rows = rows_ref[:, :features]
    all_ref[...] = rows
    spare = out_ref.shape[1] - hidden
    out_ref[:, :hidden] = dot(rows, down_ref[...], NT)
    with_bias = jnp.sum(rows.astype(F32) * bias_ref[...], axis=1, keepdims=True)
    out_ref[:, hidden:] = jnp.broadcast_to(with_bias, (rows.shape[0], spare))


def grad_hidden_product(place, chunks, down, bias):
    count, chunk = chunks[0].shape
    hidden, features = down.shape
    width = round_up(hidden + 1, 128)
    block = count // 4
    return pl.pallas_call(
        grad_hidden_kernel,
        grid=(count // block,),
        out_shape=(
            jax.ShapeDtypeStruct((count, width), F32),
            jax.ShapeDtypeStruct((count, features), LOW),
        ),
        in_specs=[IN_SMEM]
        + [by_row(block, chunk)] * len(chunks)
        + [whole_block(hidden, features), whole_block(1, features)],
        out_specs=(by_row(block, width), by_row(block, features)),
        scratch_shapes=[pltpu.VMEM((block, len(chunks) * chunk), LOW)],
        compiler_params=kernel_params(),
        cost_estimate=SHORT,
        name="grad_hidden",
    )(place, *chunks, down, bias)


def result_kernel(act_ref, down_ref, bias_ref, out_ref):
    parts, rows, width = out_ref.shape
    result = (dot(act_ref[...], down_ref[...]) + bias_ref[...]).astype(LOW)
    for part in range(parts):
        columns = result[:, part * width : (part + 1) * width]
        out_ref[part, :, : columns.shape[1]] = columns
        if columns.shape[1] < width:
            out_ref[part, :, columns.shape[1] :] = jnp.zeros((rows, width - columns.shape[1]), LOW)


def expert_result(act, down, bias, parts, width):
    count, hidden = act.shape
    features = down.shape[1]
    block = count // 4
    return pl.pallas_call(
        result_kernel,
        grid=(count // block,),
        out_shape=jax.ShapeDtypeStruct((parts, count, width), LOW),
        in_specs=[by_row(block, hidden), held_block(hidden, features), whole_block(1, features)],
        out_specs=pl.BlockSpec((parts, block, width), lambda i: (0, i, 0)),
        compiler_params=kernel_params(),
        cost_estimate=SHORT,
        name="expert_result",
    )(act, down, bias)


def place_kernel(place_ref, rows_ref, out_ref):
    out_ref[...] = dot(place_ref[...], rows_ref[...]).astype(LOW)


def place_rows(place, rows):
    count, tokens = place.shape
    width = rows.shape[1]
    block = count // 4
    return pl.pallas_call(
        place_kernel,
        grid=(count // block,),
        out_shape=jax.ShapeDtypeStruct((count, width), LOW),
        in_specs=[
            pl.BlockSpec((block, tokens), lambda i: (i, 0)),
            pl.BlockSpec((tokens, width), lambda i: (0, 0)),
        ],
        out_specs=pl.BlockSpec((block, width), lambda i: (i, 0)),
        compiler_params=kernel_params(),
        cost_estimate=SHORT,
        name="place_rows",
    )(place, rows)


def expert_kernel(experts, ring, place_ref, *refs):
    near_refs, refs = refs[:ring], refs[ring:]
    far_ref, first_ref, gate_ref, up_ref, gate_bias_ref, up_bias_ref, mine_ref = refs[:7]
    grad_far_ref, act_ref, act_gated_ref, grad_gate_ref, grad_up_ref = refs[7:12]
    bias_sums_ref, rows_ref, near_ref = refs[12:]
    hidden, features = gate_ref.shape
    split = near_ref.shape[1]
    rest = features - split
    assemble(place_ref, near_refs, near_ref)
    near, far = near_ref[...], far_ref[:, :rest]
    rows_ref[:, :split], rows_ref[:, split:] = near, far
    mine = mine_ref[...]
    gate = jnp.sum(far_ref[:, rest:].astype(F32) * mine, axis=1, keepdims=True)

    def product(weights_ref):
        return dot(near, weights_ref[:, :split], NT) + dot(far, weights_ref[:, split:], NT)

    gate_lin = product(gate_ref) + gate_bias_ref[...]
    up_lin = product(up_ref) + up_bias_ref[...]
    gate_tanh = jnp.tanh(gate_lin * (1.0 / CLAMP_LIMIT))
    up_tanh = jnp.tanh(up_lin * (1.0 / CLAMP_LIMIT))
    gate_soft = CLAMP_LIMIT * gate_tanh
    up_one = CLAMP_LIMIT * up_tanh + 1.0
    sigmoid = 1.0 / (1.0 + jnp.exp(-GLU_SLOPE * gate_soft))
    swish = gate_soft * sigmoid
    act = (up_one * swish).astype(LOW)
    act_ref[...] = act
    act_gated_ref[:, :hidden] = (act.astype(F32) * gate).astype(LOW)
    spare = act_gated_ref.shape[1] - hidden
    act_gated_ref[:, hidden:] = jnp.broadcast_to(gate.astype(LOW), (act.shape[0], spare))
    first = first_ref[:, :hidden]
    with_bias = jnp.max(first_ref[:, hidden:], axis=1, keepdims=True)
    grad_weight = jnp.sum(act.astype(F32) * first, axis=1, keepdims=True) + with_bias
    grad_act = first * gate
    swish_slope = sigmoid + GLU_SLOPE * swish * (1.0 - sigmoid)
    grad_gate = (grad_act * up_one * swish_slope * (1.0 - gate_tanh * gate_tanh)).astype(LOW)
    grad_up = (grad_act * swish * (1.0 - up_tanh * up_tanh)).astype(LOW)
    grad_gate_ref[...] = grad_gate
    grad_up_ref[...] = grad_up
    grad_far = dot(grad_gate, gate_ref[:, split:]) + dot(grad_up, up_ref[:, split:])
    grad_far_ref[:, :rest] = grad_far.astype(LOW)
    high = grad_weight.astype(LOW).astype(F32)
    lanes = lane_index(mine.shape)
    spread = jnp.where(lanes < experts, high, grad_weight - high) * mine
    grad_far_ref[:, rest:] = spread.astype(LOW)
    sums = jnp.concatenate(
        [
            jnp.sum(grad_gate.astype(F32), axis=0, keepdims=True),
            jnp.sum(grad_up.astype(F32), axis=0, keepdims=True),
        ],
        axis=0,
    )
    is_first = pl.program_id(0) == 0
    bias_sums_ref[...] = jnp.where(is_first, 0.0, bias_sums_ref[...]) + sums


def expert_step(place, near, far, first, gate, up, gate_bias, up_bias, mine, experts):
    count = far.shape[0]
    hidden, features = gate.shape
    block = count // 4
    rest = features - sum(one.shape[1] for one in near)
    gated = round_up(hidden + 8, 128)
    hidden_rows = jax.ShapeDtypeStruct((count, hidden), LOW)
    return pl.pallas_call(
        functools.partial(expert_kernel, experts, len(near)),
        grid=(count // block,),
        out_shape=(
            jax.ShapeDtypeStruct(far.shape, LOW),
            hidden_rows,
            jax.ShapeDtypeStruct((count, gated), LOW),
            hidden_rows,
            hidden_rows,
            jax.ShapeDtypeStruct((2, hidden), F32),
            jax.ShapeDtypeStruct((count, features), LOW),
        ),
        in_specs=[IN_SMEM]
        + [by_row(block, one.shape[1]) for one in near]
        + [
            by_row(block, far.shape[1]),
            by_row(block, first.shape[1]),
            held_block(hidden, features),
            held_block(hidden, features),
            whole_block(1, hidden),
            whole_block(1, hidden),
            whole_block(1, mine.shape[1]),
        ],
        out_specs=(
            by_row(block, far.shape[1]),
            by_row(block, hidden),
            by_row(block, gated),
            by_row(block, hidden),
            by_row(block, hidden),
            whole_block(2, hidden),
            by_row(block, features),
        ),
        scratch_shapes=[pltpu.VMEM((block, features - rest), LOW)],
        compiler_params=kernel_params(),
        cost_estimate=pl.CostEstimate(
            flops=8 * count * features * hidden,
            bytes_accessed=8 * count * features + 4 * features * hidden + 12 * count * hidden,
            transcendentals=3 * count * hidden,
        ),
        name="expert_step",
    )(place, *near, far, first, gate, up, gate_bias, up_bias, mine)


def grad_rows_kernel(grad_gate_ref, grad_up_ref, gate_ref, up_ref, out_ref):
    out = dot(grad_gate_ref[...], gate_ref[...]) + dot(grad_up_ref[...], up_ref[...])
    out_ref[...] = out.astype(LOW)


def grad_rows_near(grad_gate, grad_up, gate, up, split):
    count, hidden = grad_gate.shape
    block = count // 4
    return pl.pallas_call(
        grad_rows_kernel,
        grid=(count // block,),
        out_shape=jax.ShapeDtypeStruct((count, split), LOW),
        in_specs=[
            by_row(block, hidden),
            by_row(block, hidden),
            held_block(hidden, split),
            held_block(hidden, split),
        ],
        out_specs=by_row(block, split),
        compiler_params=kernel_params(),
        cost_estimate=SHORT,
        name="grad_rows",
    )(grad_gate, grad_up, gate, up)


def weight_grad_kernel(left_ref, right_ref, out_ref, *refs):
    bias_ref, turned_ref = refs if len(refs) == 2 else (None, refs[0])

    @pl.when(pl.program_id(0) == 0)
    def _():
        turned_ref[...] = left_ref[...].T

    hidden = out_ref.shape[0]
    product = dot(turned_ref[...], right_ref[...])
    out_ref[...] = product[:hidden]
    if bias_ref is not None:
        bias_ref[...] = product[hidden : hidden + 8]


def weight_grad(left, right, hidden):
    count, width = left.shape
    features = right.shape[1]
    block = round_up(-(-features // STEPS), 128)
    out_shape = [jax.ShapeDtypeStruct((hidden, features), F32)]
    out_specs = [by_column(hidden, block)]
    if width > hidden:
        out_shape.append(jax.ShapeDtypeStruct((8, features), F32))
        out_specs.append(by_column(8, block))
    return pl.pallas_call(
        weight_grad_kernel,
        grid=(STEPS,),
        out_shape=out_shape,
        in_specs=[whole_block(count, width), by_column(count, block)],
        out_specs=out_specs,
        scratch_shapes=[pltpu.VMEM((width, count), LOW)],
        compiler_params=kernel_params(),
        cost_estimate=SHORT,
        name="weight_grad",
    )(left, right)


def exchange(rows, parts):
    count, width = rows.shape
    moved = lax.all_to_all(
        rows.reshape(parts, count // parts, width),
        "expert",
        split_axis=0,
        concat_axis=0,
        tiled=True,
    )
    return moved.reshape(count, width)


def low_sum(halves):
    upper, upper_in, lower, lower_in = halves
    return (
        (upper.astype(F32) + upper_in.astype(F32)).astype(LOW),
        (lower.astype(F32) + lower_in.astype(F32)).astype(LOW),
    )


def tensor_sum(upper, lower, ring, middle=low_sum):
    near = [(i, i ^ 1) for i in range(ring)]
    far = [(i, ring - 1 - i) for i in range(ring)]
    upper_in = lax.ppermute(upper, "tensor", near)
    lower_in = lax.ppermute(lower, "tensor", far)
    upper, lower = middle((upper, upper_in, lower, lower_in))
    upper_in = lax.ppermute(upper, "tensor", far)
    lower_in = lax.ppermute(lower, "tensor", near)
    return upper, upper_in, lower, lower_in


def together(*values):
    return lax.optimization_barrier(values)


def ring_steps(ring):
    return [(i, (i + 1) % ring) for i in range(ring)], [(i, (i - 1) % ring) for i in range(ring)]


def tensor_chunks(own, ring):
    up, down = ring_steps(ring)
    half = own.shape[0] // 2
    before = lax.ppermute(own, "tensor", up)
    behind = lax.ppermute(own, "tensor", down)
    far_top = lax.ppermute(before[:half], "tensor", up)
    far_bottom = lax.ppermute(behind[half:], "tensor", down)
    across = jnp.concatenate([far_top, far_bottom], axis=0)
    return own, behind, across, before


def tensor_chunks_short(own, ring):
    across = [(i, (i + 2) % ring) for i in range(ring)]
    up, down = ring_steps(ring)
    before = lax.ppermute(own, "tensor", up)
    behind = lax.ppermute(own, "tensor", down)
    return own, behind, lax.ppermute(own, "tensor", across), before


def expert_sum(values, count, beside, work):
    masks = {32: (1, 2, 6, 8, 24)}.get(count) or [1 << i for i in range(count.bit_length() - 1)]
    for step, mask in enumerate(masks):
        if step == len(masks) // 2:
            values, beside = together(values, beside)
            made = work(beside)
        if step == len(masks) - 1:
            values, made = together(values, made)
        there = lax.ppermute(values, "expert", [(i, i ^ mask) for i in range(count)])
        values = (values.astype(F32) + there.astype(F32)).astype(values.dtype)
    return values, beside, made


def on_device(
    expert_axis,
    tensor_axis,
    block_input,
    out_cotangent,
    seq_lengths,
    route_ids,
    attn_gain,
    w_query,
    w_key,
    w_value,
    b_query,
    b_key,
    b_value,
    sink_logits,
    w_output,
    b_output,
    ffn_gain,
    w_router,
    b_router,
    w_gate,
    w_up,
    b_gate,
    b_up,
    w_down,
    b_down,
):
    tokens, features = block_input.shape
    heads = sink_logits.shape[0]
    experts = w_router.shape[1]
    capacity = 2 * tokens * route_ids.shape[1] // experts
    slots = experts * capacity
    shard = w_query.shape[0]
    shard_pad = round_up(shard + 1, 16)
    width = round_up(features + 2 * experts, 128)
    chunk = max(1, round(width / 128 / (2 * tensor_axis))) * 128
    split = chunk * tensor_axis
    rest = features - split
    block_width = round_up(-(-features // tensor_axis), 128)
    mine_expert = lax.axis_index("expert")
    mine_tensor = lax.axis_index("tensor")

    out_width = w_output.shape[0]
    packed = jnp.concatenate([w_output.T, w_query, w_key, w_value], axis=1)
    packed = jnp.pad(packed, ((0, shard_pad - shard), (0, 0)))
    weights = lax.all_gather(packed, "expert", axis=0, tiled=True)

    expert_ids = jnp.arange(experts, dtype=jnp.int32)
    named = jnp.any(route_ids[:, :, None] == expert_ids[None, None, :], axis=1)
    named_t = jnp.any(route_ids.T[:, None, :] == expert_ids[None, :, None], axis=0)
    token_ids = jnp.arange(tokens, dtype=jnp.int32)
    earlier = (token_ids[:, None] < token_ids[None, :]).astype(LOW)
    rank_t = dot(named_t.astype(LOW), earlier).astype(jnp.int32)
    place = (rank_t[:, None, :] == jnp.arange(capacity, dtype=jnp.int32)[None, :, None]) & named_t[
        :, None, :
    ]
    place = place.astype(LOW).reshape(slots, tokens)
    place_t = place.T


    def own_block(rows, size, ahead=0):
        start = (mine_tensor + ahead) % tensor_axis * size
        return lax.dynamic_slice(rows, (0, start), (tokens, size))

    cotangent_wide = jnp.pad(
        out_cotangent, ((0, 0), (0, block_width * tensor_axis - features))
    )
    cotangent_own = exchange(place_rows(place, own_block(cotangent_wide, block_width)), experts)
    up, down_ring = ring_steps(tensor_axis)
    cotangent_before = lax.ppermute(cotangent_own, "tensor", up)
    cotangent_behind = lax.ppermute(cotangent_own, "tensor", down_ring)
    cotangent_across = place_rows(place, own_block(cotangent_wide, block_width, 2))

    segment, position = layout(seq_lengths[0], tokens)
    cos, sin = rope_tables(position)
    allowed = (segment[:, None] == segment[None, :]) & (token_ids[None, :] <= token_ids[:, None])
    allowed = allowed.astype(F32)

    inputs = block_input.astype(F32)
    scale_one = lax.rsqrt(jnp.mean(inputs * inputs, axis=-1, keepdims=True) + EPSILON)
    unit_one = inputs * scale_one
    normed_low = (unit_one * attn_gain).astype(LOW)
    spread_low = jnp.pad(
        normed_low.reshape(tokens, expert_axis, shard), ((0, 0), (0, 0), (0, shard_pad - shard))
    )
    one_column = (jnp.arange(shard_pad) == shard).astype(LOW)
    normed_blocks = jnp.transpose(spread_low + one_column, (1, 2, 0))
    normed_blocks = normed_blocks.reshape(expert_axis * shard_pad, tokens)

    (
        weights,
        cotangent_across,
        cotangent_own,
        cotangent_before,
        cotangent_behind,
        normed_blocks,
    ) = together(
        weights,
        cotangent_across,
        cotangent_own,
        cotangent_before,
        cotangent_behind,
        normed_blocks,
    )
    cotangent_across = exchange(cotangent_across, experts)
    bias = jnp.concatenate([b_query, b_key, b_value])[None, :]
    spread_low = spread_low.reshape(tokens, expert_axis * shard_pad)
    attn_low, rotated, lse = attend_forward(
        sink_logits, spread_low, weights, bias, cos, sin, allowed
    )
    attn_all = lax.all_gather(attn_low, "expert", axis=0, tiled=True)
    attn_part = compact_product(attn_low, tokens, weights, out_width, shard, shard_pad, "attn_output")
    attn_sum = tensor_sum(*attn_part, tensor_axis)
    ring_place = mine_tensor.astype(jnp.int32).reshape(1)
    residual, gates, sent, rows_own = token_forward(
        ring_place,
        block_input,
        attn_sum,
        b_output[None, :],
        ffn_gain[None, :],
        w_router.T,
        b_router[None, :],
        named.astype(F32),
        place,
        width,
        chunk,
    )

    gate_t, up_t, down = w_gate[0].T, w_up[0].T, w_down[0]
    hidden = down.shape[0]
    bias_once = jnp.where(mine_tensor == 0, b_down, 0.0)
    rows_own, cotangent_across = together(rows_own, cotangent_across)
    cotangent_rows = (cotangent_own, cotangent_behind, cotangent_across, cotangent_before)
    first, cotangent_all = grad_hidden_product(ring_place, cotangent_rows, down, bias_once)
    rows_own = exchange(rows_own, experts)
    rows_far = place_rows(place, sent[:, split:])
    rows_own, rows_far, first = together(rows_own, rows_far, first)
    rows_near = tensor_chunks(rows_own, tensor_axis)
    rows_far = exchange(rows_far, experts)

    lane = jnp.arange(width - features)
    mine = ((lane % experts == mine_expert) & (lane < 2 * experts)).astype(F32)[None, :]
    rows_near, rows_far, attn_all = together(rows_near, rows_far, attn_all)
    grad_far, act, act_gated, grad_gate, grad_up, bias_sums, rows_all = expert_step(
        ring_place, rows_near, rows_far, first, gate_t, up_t, b_gate, b_up, mine, experts
    )
    back_far = exchange(grad_far, experts)
    grad_near = grad_rows_near(grad_gate, grad_up, gate_t, up_t, split)
    result = expert_result(act, down, bias_once, tensor_axis, block_width)
    result_own = lax.psum_scatter(result, "tensor", scatter_dimension=0, tiled=False)
    grad_near, back_far, grad_gate, grad_up, act_gated = together(
        grad_near, back_far, grad_gate, grad_up, act_gated
    )
    back_near = exchange(grad_near, experts)
    far_halves = combine_far(place_t, back_far, rest, experts)
    w_gate_grad = weight_grad(grad_gate, rows_all, hidden)[0]

    def middle(halves):
        nonlocal w_gate_grad, grad_up, act_gated
        *halves, w_gate_grad = together(*halves, w_gate_grad)
        upper, lower = middle_far(halves, rest, experts)
        upper, lower, grad_up, act_gated = together(upper, lower, grad_up, act_gated)
        return upper, lower

    far_sum = tensor_sum(*far_halves, tensor_axis, middle)
    w_up_grad = weight_grad(grad_up, rows_all, hidden)[0]
    w_down_grad, b_down_grad = weight_grad(act_gated, cotangent_all, hidden)
    back_near, w_up_grad, w_down_grad, b_down_grad, result_own, *far_sum = together(
        back_near, w_up_grad, w_down_grad, b_down_grad, result_own, *far_sum
    )
    w_gate_grad, w_up_grad = w_gate_grad.T[None], w_up_grad.T[None]
    w_down_grad, b_down_grad = w_down_grad[None], b_down_grad[0:1]
    b_gate_grad = bias_sums[0:1]
    b_up_grad = bias_sums[1:2]

    upper, lower = combine_near(place_t, back_near)
    upper, lower, result_own = together(upper, lower, result_own)
    near_sum = tensor_sum(upper, lower, tensor_axis)
    returned = exchange(result_own, experts)
    grad_resid, resid_spread, resid_blocks, router_block, vectors = token_backward(
        ring_place,
        near_sum,
        far_sum,
        gates,
        w_router.T,
        residual,
        out_cotangent,
        ffn_gain[None, :],
        shard,
        shard_pad,
        tensor_axis,
    )
    grad_qkv, sink_part = attend_backward(
        sink_logits, resid_spread, weights, rotated, lse, cos, sin, allowed
    )
    grad_qkv, returned = together(grad_qkv, returned)
    grad_qkv_all = lax.all_gather(grad_qkv, "expert", axis=0, tiled=True)
    upper, lower, attn_gain_part = compact_product(
        grad_qkv, tokens, weights, weights.shape[1], shard, shard_pad, "grad_normed", spread_low
    )
    grad_normed = tensor_sum(upper, lower, tensor_axis)
    normed_blocks = normed_blocks.reshape(expert_axis, shard_pad, tokens)
    blocks = jnp.concatenate([normed_blocks, resid_blocks], axis=1)
    blocks = exchange(blocks.reshape(expert_axis * 2 * shard_pad, tokens), expert_axis)
    blocks = blocks.reshape(expert_axis, 2 * shard_pad, tokens)

    sinks_row = jnp.pad(sink_part[:, :heads], ((0, 0), (0, tokens - heads)))
    small = pack_small(router_block, vectors, attn_gain_part, sinks_row)

    def output_product(blocks):
        return gathered_products(
            blocks, 1, attn_all, (out_width,), shard, shard_pad, False, "output_grad"
        )[0]

    small, blocks, w_output_grad = expert_sum(small, expert_axis, blocks, output_product)
    small, returned = together(small, returned)
    shared = experts + -(-features // block_width)
    widths = (w_query.shape[1], w_key.shape[1], w_value.shape[1])
    w_output_grad = w_output_grad.T
    qkv_grads = gathered_products(
        blocks, 0, grad_qkv_all, widths, shard, shard_pad, True, "qkv_grad"
    )
    query_grad, *qkv_grads = qkv_grads
    chunks = tensor_chunks_short(small[:shared], tensor_axis)
    router_grad, gain_grad, ffn_gain_grad, output_bias_grad, sink_grad, router_bias_grad = (
        unpack_small(ring_place, chunks, small[shared:], attn_gain[None, :], experts, heads)
    )

    input_grad = input_grad_rows(grad_normed, grad_resid, block_input, attn_gain[None, :]).T
    mixed = tensor_chunks_short(mix_results(place_t, gates, returned), tensor_axis)
    block_output = output_rows(ring_place, mixed, residual).T

    return (
        block_output,
        input_grad,
        gain_grad,
        query_grad,
        qkv_grads[0],
        qkv_grads[1],
        qkv_grads[2],
        qkv_grads[3],
        qkv_grads[4],
        sink_grad,
        w_output_grad,
        output_bias_grad,
        ffn_gain_grad,
        router_grad.T,
        router_bias_grad,
        w_gate_grad,
        w_up_grad,
        b_gate_grad,
        b_up_grad,
        w_down_grad,
        b_down_grad,
    )


def solution(mesh):
    in_specs = (
        P("expert", None),
        P("expert", None),
        P("expert", None),
        P("expert", None),
        P(),
        P("expert", "tensor"),
        P("expert", "tensor"),
        P("expert", "tensor"),
        P("tensor"),
        P("tensor"),
        P("tensor"),
        P("tensor"),
        P("tensor", "expert"),
        P(),
        P(),
        P(),
        P(),
        P("expert", None, "tensor"),
        P("expert", None, "tensor"),
        P("expert", "tensor"),
        P("expert", "tensor"),
        P("expert", "tensor", None),
        P("expert", None),
    )
    out_specs = (
        P("expert", None),
        P("expert", None),
        P(),
        P("expert", "tensor"),
        P("expert", "tensor"),
        P("expert", "tensor"),
        P("tensor"),
        P("tensor"),
        P("tensor"),
        P("tensor"),
        P("tensor", "expert"),
        P(),
        P(),
        P(),
        P(),
        P("expert", None, "tensor"),
        P("expert", None, "tensor"),
        P("expert", "tensor"),
        P("expert", "tensor"),
        P("expert", "tensor", None),
        P("expert", None),
    )
    body = functools.partial(on_device, mesh.shape["expert"], mesh.shape["tensor"])
    return jax.shard_map(body, mesh=mesh, in_specs=in_specs, out_specs=out_specs, check_vma=False)
```

profile of v0, /device:TPU:32, one launch (start us, length us, event | category | flops | bytes accessed | tf_op | source)
XLA Modules:
  0.0 489.4 jit_solution(17696372772327424767)
XLA Ops:
  16.0 7.5 %all-to-all-start = ((bf16[32,32,768]{2,1,0:T(8,128)(2,1)}), bf16[32,32,768]{2,1,0:T(8,128)(2,1)S(1)}, u32[]{:S(2)}, u32[]{:S(2)}) async-start(bf16[32,32,768]{2,1,0:T(8,128)(2,1)} %bitcast.63), calls=%async_computation | async-start | bytes 3145728 | tf_op jit(solution)/shard_map/all_to_all | solution.py:1068
  23.9 28.8 %all-to-all-done = bf16[32,32,768]{2,1,0:T(8,128)(2,1)S(1)} async-done(((bf16[32,32,768]{2,1,0:T(8,128)(2,1)}), bf16[32,32,768]{2,1,0:T(8,128)(2,1)S(1)}, u32[]{:S(2)}, u32[]{:S(2)}) %all-to-all-start) | async-done | bytes 1572896 | tf_op jit(solution)/shard_map/all_to_all | solution.py:1068
  67.8 20.1 %collective-permute-done.refs_3_ = bf16[1024,768]{1,0:T(8,128)(2,1)} collective-permute-done((bf16[1024,768]{1,0:T(8,128)(2,1)S(1)}, bf16[1024,768]{1,0:T(8,128)(2,1)}, u32[]{:S(2)}, u32[]{:S(2)}) %collective-permute-start) | collective-permute-done | bytes 1572896 | tf_op jit(solution)/shard_map/ppermute | solution.py:1206
  92.5 13.0 %attend_forward.1 = (bf16[128,1024]{1,0:T(8,128)(2,1)}, bf16[128,1280]{1,0:T(8,128)(2,1)}, f32[128,128]{1,0:T(8,128)}) custom-call(f32[16]{0:T(128)} %sink_ref.3, bf16[128,3072]{1,0:T(8,128)(2,1)} %copy.88.rows_ref.refs_0_, bf16[3072,2304]{1,0:T(8,128)(2,1)} %all-gather.4.cloned.1.call-done.weights_ref, f32[1,1280]{1,0:T(1,128)} %broadcast_in_dim.34.bias_ref, ...), custom_call_target="tpu_custom_call" | custom-call | flops 1 | bytes 1 | tf_op jit(solution)/shard_map/attend_forward/pallas_call | solution.py:284
  105.5 6.4 %attn_output.1 = (bf16[64,2880]{1,0:T(8,128)(2,1)}, bf16[64,2880]{1,0:T(8,128)(2,1)}) custom-call(bf16[128,1024]{1,0:T(8,128)(2,1)} %get-tuple-element.121.left_ref, bf16[3072,2304]{1,0:T(8,128)(2,1)} %all-gather.4.cloned.1.call-done.weights_ref), custom_call_target="tpu_custom_call" | custom-call | flops 1 | bytes 1 | tf_op jit(solution)/shard_map/attn_output/pallas_call | solution.py:377
  115.3 5.5 %all-to-all-start.1 = ((bf16[32,32,768]{2,1,0:T(8,128)(2,1)}), bf16[32,32,768]{2,1,0:T(8,128)(2,1)S(1)}, u32[]{:S(2)}, u32[]{:S(2)}) async-start(bf16[32,32,768]{2,1,0:T(8,128)(2,1)} %bitcast.16), calls=%async_computation.1 | async-start | bytes 3145728 | tf_op jit(solution)/shard_map/all_to_all | solution.py:1068
  138.9 5.5 %token_forward.1 = (f32[128,2880]{1,0:T(8,128)}, f32[128,32]{1,0:T(8,128)}, bf16[128,2944]{1,0:T(8,128)(2,1)}, bf16[1024,384]{1,0:T(8,128)(2,1)}) custom-call(s32[1]{0:T(128)} %bitcast.place_ref, bf16[128,2880]{1,0:T(8,128)(2,1)} %copy.89.input_ref.refs_5_, bf16[64,2880]{1,0:T(8,128)(2,1)} %copy-done.14, bf16[64,2880]{1,0:T(8,128)(2,1)} %copy-done.25, ...), custom_call_target="tpu_custom_call" | custom-call | flops 1 | bytes 1 | tf_op jit(solution)/shard_map/token_forward/pallas_call | solution.py:434
  145.4 4.4 all-to-all-start.2
  152.2 4.3 place_rows.5
  156.5 10.5 %grad_hidden.1 = (f32[1024,768]{1,0:T(8,128)}, bf16[1024,2880]{1,0:T(8,128)(2,1)}) custom-call(s32[1]{0:T(128)} %bitcast.place_ref, bf16[1024,768]{1,0:T(8,128)(2,1)} %bitcast.66, bf16[1024,768]{1,0:T(8,128)(2,1)} %collective-permute-done.1.refs_1_, bf16[1024,768]{1,0:T(8,128)(2,1)} %bitcast.67, bf16[1024,768]{1,0:T(8,128)(2,1)} %collective-permute-done.refs_3_, ...), custom_call_target="tpu_custom_call" | custom-call | flops 1 | bytes 1 | tf_op jit(solution)/shard_map/grad_hidden/pallas_call | solution.py:832
  167.0 6.1 %all-to-all-done.2 = bf16[32,32,384]{2,1,0:T(8,128)(2,1)S(1)} async-done(((bf16[32,32,384]{2,1,0:T(8,128)(2,1)}), bf16[32,32,384]{2,1,0:T(8,128)(2,1)S(1)}, u32[]{:S(2)}, u32[]{:S(2)}) %all-to-all-start.2) | async-done | bytes 786464 | tf_op jit(solution)/shard_map/all_to_all | solution.py:1068
  173.9 4.1 all-to-all-start.3
  180.1 17.8 %collective-permute-done.7.refs_3_ = bf16[1024,384]{1,0:T(8,128)(2,1)S(1)} collective-permute-done((bf16[1024,384]{1,0:T(8,128)(2,1)}, bf16[1024,384]{1,0:T(8,128)(2,1)S(1)}, u32[]{:S(2)}, u32[]{:S(2)}) %collective-permute-start.7) | collective-permute-done | bytes 786464 | tf_op jit(solution)/shard_map/ppermute | solution.py:1108
  203.7 5.6 %collective-permute-done.8 = bf16[512,384]{1,0:T(8,128)(2,1)} collective-permute-done((bf16[512,384]{1,0:T(8,128)(2,1)S(1)}, bf16[512,384]{1,0:T(8,128)(2,1)}, u32[]{:S(2)}, u32[]{:S(2)}) %collective-permute-start.8) | collective-permute-done | bytes 393248 | tf_op jit(solution)/shard_map/ppermute | solution.py:1110
  218.4 22.8 %expert_step.1 = (bf16[1024,1408]{1,0:T(8,128)(2,1)}, bf16[1024,720]{1,0:T(8,128)(2,1)}, bf16[1024,768]{1,0:T(8,128)(2,1)}, bf16[1024,720]{1,0:T(8,128)(2,1)}, b...) custom-call(s32[1]{0:T(128)} %bitcast.place_ref, bf16[1024,384]{1,0:T(8,128)(2,1)} %bitcast.83, ...), custom_call_target="tpu_custom_call" | custom-call | flops 16986931200 | bytes 40734720 | tf_op jit(solution)/shard_map/expert_step/pallas_call | solution.py:962
  241.2 9.2 %expert_result.1 = bf16[4,1024,768]{2,1,0:T(8,128)(2,1)} custom-call(bf16[1024,720]{1,0:T(8,128)(2,1)} %get-tuple-element.165.act_ref, bf16[720,2880]{1,0:T(8,128)(2,1)} %bitcast.53, f32[1,2880]{1,0:T(1,128)} %broadcast_select_fusion.refs_5_.bias_ref), custom_call_target="tpu_custom_call" | custom-call | flops 1 | bytes 1 | tf_op jit(solution)/shard_map/expert_result/pallas_call | solution.py:864
  250.4 4.6 all-to-all-start.4
  255.1 9.3 %grad_rows.1 = bf16[1024,1536]{1,0:T(8,128)(2,1)} custom-call(bf16[1024,720]{1,0:T(8,128)(2,1)} %get-tuple-element.150.grad_gate_ref.left_ref, bf16[1024,720]{1,0:T(8,128)(2,1)} %get-tuple-element.160.grad_up_ref.left_ref, bf16[720,2880]{1,0:T(8,128)(2,1)} %bitcast.69, bf16[720,2880]{1,0:T(8,128)(2,1)} %bitcast.71), custom_call_target="tpu_custom_call" | custom-call | flops 1 | bytes 1 | tf_op jit(solution)/shard_map/grad_rows/pallas_call | solution.py:1013
  264.3 29.6 %all-to-all-done.4 = bf16[32,32,1408]{2,1,0:T(8,128)(2,1)S(1)} async-done(((bf16[32,32,1408]{2,1,0:T(8,128)(2,1)}), bf16[32,32,1408]{2,1,0:T(8,128)(2,1)S(1)}, u32[]{:S(2)}, u32[]{:S(2)}) %all-to-all-start.4) | async-done | bytes 2883616 | tf_op jit(solution)/shard_map/all_to_all | solution.py:1068
  295.5 4.1 all-to-all-start.5
  307.6 9.8 %weight_grad.3 = f32[720,2880]{1,0:T(8,128)} custom-call(bf16[1024,720]{1,0:T(8,128)(2,1)} %get-tuple-element.150.grad_gate_ref.left_ref, bf16[1024,2880]{1,0:T(8,128)(2,1)} %get-tuple-element.151.right_ref), custom_call_target="tpu_custom_call" | custom-call | flops 1 | bytes 1 | tf_op jit(solution)/shard_map/weight_grad/pallas_call | solution.py:1053
  322.3 9.8 %weight_grad.4 = f32[720,2880]{1,0:T(8,128)} custom-call(bf16[1024,720]{1,0:T(8,128)(2,1)} %get-tuple-element.160.grad_up_ref.left_ref, bf16[1024,2880]{1,0:T(8,128)(2,1)} %get-tuple-element.151.right_ref), custom_call_target="tpu_custom_call" | custom-call | flops 1 | bytes 1 | tf_op jit(solution)/shard_map/weight_grad/pallas_call | solution.py:1053
  332.1 10.1 %weight_grad.5 = (f32[720,2880]{1,0:T(8,128)}, f32[8,2880]{1,0:T(8,128)}) custom-call(bf16[1024,768]{1,0:T(8,128)(2,1)} %get-tuple-element.161.left_ref, bf16[1024,2880]{1,0:T(8,128)(2,1)} %get-tuple-element.162.right_ref), custom_call_target="tpu_custom_call" | custom-call | flops 1 | bytes 1 | tf_op jit(solution)/shard_map/weight_grad/pallas_call | solution.py:1053
  347.2 7.2 %all-to-all-start.6 = ((bf16[32,32,768]{2,1,0:T(8,128)(2,1)}), bf16[32,32,768]{2,1,0:T(8,128)(2,1)S(1)}, u32[]{:S(2)}, u32[]{:S(2)}) async-start(bf16[32,32,768]{2,1,0:T(8,128)(2,1)} %bitcast.77), calls=%async_computation.7 | async-start | bytes 3145728 | tf_op jit(solution)/shard_map/all_to_all | solution.py:1068
  371.2 6.8 %token_backward.1 = (f32[128,2880]{1,0:T(8,128)}, bf16[128,3072]{1,0:T(8,128)(2,1)}, bf16[32,96,128]{2,1,0:T(8,128)(2,1)}, bf16[32,768]{1,0:T(8,128)(2,1)}, f32[8,3072]{1,0:T(8,128)}) custom-call(s32[1]{0:T(128)} %bitcast.place_ref, bf16[64,1536]{1,0:T(8,128)(2,1)} %copy-done.16, bf16[64,1536]{1,0:T(8,128)(2,1)} %copy-done.28, bf16[64,1536]{1,0:T(8,128)(2,1)} %copy-done.15, ...), custom_call_target="tpu_custom_call" | custom-call | flops 1 | bytes 1 | tf_op jit(solution)/shard_map/token_backward/pallas_call | solution.py:649
  378.1 10.8 %attend_backward.1 = (bf16[128,1280]{1,0:T(8,128)(2,1)}, f32[1,128]{1,0:T(1,128)}) custom-call(f32[16]{0:T(128)} %sink_ref.3, bf16[128,3072]{1,0:T(8,128)(2,1)} %get-tuple-element.181.rows_ref, bf16[3072,2304]{1,0:T(8,128)(2,1)} %all-gather.4.cloned.1.call-done.weights_ref, bf16[128,1280]{1,0:T(8,128)(2,1)} %get-tuple-element.182.rot_ref, ...), custom_call_target="tpu_custom_call" | custom-call | flops 1 | bytes 1 | tf_op jit(solution)/shard_map/attend_backward/pallas_call | solution.py:318
  390.6 7.5 %all-to-all-start.7 = ((bf16[32,192,128]{2,1,0:T(8,128)(2,1)}), bf16[32,192,128]{2,1,0:T(8,128)(2,1)S(1)}, u32[]{:S(2)}, u32[]{:S(2)}) async-start(bf16[32,192,128]{2,1,0:T(8,128)(2,1)} %pad_maximum_fusion), calls=%async_computation.8 | async-start | bytes 3145728 | tf_op jit(solution)/shard_map/all_to_all | solution.py:1068
  398.7 9.7 %grad_normed.1 = (bf16[64,2880]{1,0:T(8,128)(2,1)}, bf16[64,2880]{1,0:T(8,128)(2,1)}, f32[1,2880]{1,0:T(1,128)}) custom-call(bf16[128,1280]{1,0:T(8,128)(2,1)} %get-tuple-element.186.left_ref, bf16[3072,2304]{1,0:T(8,128)(2,1)} %all-gather.4.cloned.1.call-done.weights_ref, bf16[128,3072]{1,0:T(8,128)(2,1)} %copy.88.rows_ref.refs_0_), custom_call_target="tpu_custom_call" | custom-call | flops 1 | bytes 1 | tf_op jit(solution)/shard_map/grad_normed/pallas_call | solution.py:377
  416.0 8.7 %collective-permute-done.19 = bf16[48,768]{1,0:T(8,128)(2,1)S(1)} collective-permute-done((bf16[48,768]{1,0:T(8,128)(2,1)S(1)}, bf16[48,768]{1,0:T(8,128)(2,1)S(1)}, u32[]{:S(2)}, u32[]{:S(2)}) %collective-permute-start.19) | collective-permute-done | bytes 73760 | tf_op jit(solution)/shard_map/ppermute | solution.py:1132
  435.3 6.2 %output_grad.1 = f32[90,1024]{1,0:T(8,128)} custom-call(bf16[32,192,128]{2,1,0:T(8,128)(2,1)} %copy-done, bf16[4096,1024]{1,0:T(8,128)(2,1)} %all-gather.6.cloned.1.call-done.rows_ref), custom_call_target="tpu_custom_call" | custom-call | flops 1 | bytes 1 | tf_op jit(solution)/shard_map/output_grad/pallas_call | solution.py:623
  466.8 4.3 input_grad.1
  475.5 7.0 %qkv_grad.1 = (f32[90,1024]{1,0:T(8,128)}, f32[90,128]{1,0:T(8,128)}, f32[90,128]{1,0:T(8,128)}, f32[1024]{0:T(1024)}, f32[128]{0:T(128)}, /*index=5*/f32[128]{0:T(128)}) custom-call(bf16[32,192,128]{2,1,0:T(8,128)(2,1)} %copy-done, bf16[4096,1280]{1,0:T(8,128)(2,1)} %all-gather.8.cloned.1.call-done.rows_ref), custom_call_target="tpu_custom_call" | custom-call | flops 1 | bytes 1 | tf_op jit(solution)/shard_map/qkv_grad/pallas_call | solution.py:623
  (257 shorter events, 157.5 us)
Async XLA Ops:
  7.2 85.3 %all-gather.4.cloned.1.call-start = ((), (), s32[]{:S(2)}) async-start(), calls=%async_computation.9 | async-start | bytes 14598144 | tf_op jit(solution)/shard_map/all_gather | solution.py:1182
  16.0 36.8 %all-to-all-start = ((bf16[32,32,768]{2,1,0:T(8,128)(2,1)}), bf16[32,32,768]{2,1,0:T(8,128)(2,1)S(1)}, u32[]{:S(2)}, u32[]{:S(2)}) async-start(bf16[32,32,768]{2,1,0:T(8,128)(2,1)} %bitcast.63), calls=%async_computation | async-start | bytes 3145728 | tf_op jit(solution)/shard_map/all_to_all | solution.py:1068
  23.5 193.4 %all-gather.6.cloned.1.call-start = ((), (), s32[]{:S(2)}) async-start(), calls=%async_computation.10 | async-start | bytes 8650752 | tf_op jit(solution)/shard_map/all_gather | solution.py:1247
  52.8 35.1 %collective-permute-start = (bf16[1024,768]{1,0:T(8,128)(2,1)S(1)}, bf16[1024,768]{1,0:T(8,128)(2,1)}, u32[]{:S(2)}, u32[]{:S(2)}) collective-permute-start(bf16[1024,768]{1,0:T(8,128)(2,1)S(1)} %bitcast.64), channel_id=1, source_target_pairs={{0,1},{1,2},{2,3},{3,0},{4,5},{5,6},{6,7},{7,4},{8,9},{9,10},{10,1... | collective-permute-start | bytes 4718600 | tf_op jit(solution)/shard_map/ppermute | solution.py:1206
  54.4 34.8 %collective-permute-start.1 = (bf16[1024,768]{1,0:T(8,128)(2,1)S(1)}, bf16[1024,768]{1,0:T(8,128)(2,1)}, u32[]{:S(2)}, u32[]{:S(2)}) collective-permute-start(bf16[1024,768]{1,0:T(8,128)(2,1)S(1)} %bitcast.65), channel_id=1, source_target_pairs={{0,3},{1,0},{2,1},{3,2},{4,7},{5,4},{6,5},{7,6},{8,11},{9,8},{10,9... | collective-permute-start | bytes 4718600 | tf_op jit(solution)/shard_map/ppermute | solution.py:1207
  111.9 11.2 %collective-permute-start.4 = (bf16[64,2880]{1,0:T(8,128)(2,1)}, bf16[64,2880]{1,0:T(8,128)(2,1)}, u32[]{:S(2)}, u32[]{:S(2)}) collective-permute-start(bf16[64,2880]{1,0:T(8,128)(2,1)} %get-tuple-element.123), channel_id=1, source_target_pairs={{0,3},{1,2},{2,1},{3,0},{4,7},{5,6},{6,5},{7,4},{8,11},{9,10},{10,... | collective-permute-start | bytes 1105928 | tf_op jit(solution)/shard_map/ppermute | solution.py:1090
  113.5 12.6 %collective-permute-start.2 = (bf16[64,2880]{1,0:T(8,128)(2,1)}, bf16[64,2880]{1,0:T(8,128)(2,1)}, u32[]{:S(2)}, u32[]{:S(2)}) collective-permute-start(bf16[64,2880]{1,0:T(8,128)(2,1)} %get-tuple-element.122), channel_id=1, source_target_pairs={{0,1},{1,0},{2,3},{3,2},{4,5},{5,4},{6,7},{7,6},{8,9},{9,8},{10,11... | collective-permute-start | bytes 1105928 | tf_op jit(solution)/shard_map/ppermute | solution.py:1089
  115.3 30.0 %all-to-all-start.1 = ((bf16[32,32,768]{2,1,0:T(8,128)(2,1)}), bf16[32,32,768]{2,1,0:T(8,128)(2,1)S(1)}, u32[]{:S(2)}, u32[]{:S(2)}) async-start(bf16[32,32,768]{2,1,0:T(8,128)(2,1)} %bitcast.16), calls=%async_computation.1 | async-start | bytes 3145728 | tf_op jit(solution)/shard_map/all_to_all | solution.py:1068
  127.1 11.0 %collective-permute-start.3 = (bf16[64,2880]{1,0:T(8,128)(2,1)S(1)}, bf16[64,2880]{1,0:T(8,128)(2,1)S(1)}, u32[]{:S(2)}, u32[]{:S(2)}) collective-permute-start(bf16[64,2880]{1,0:T(8,128)(2,1)S(1)} %add_convert_fusion.3.refs_0_), channel_id=1, source_target_pairs={{0,3},{1,2},{2,1},{3,0},{4,7},{5,6},{6,5},{7,4},{8,11},{9,10},{10,... | collective-permute-start | bytes 1105928 | tf_op jit(solution)/shard_map/ppermute | solution.py:1092
  145.4 27.6 %all-to-all-start.2 = ((bf16[32,32,384]{2,1,0:T(8,128)(2,1)}), bf16[32,32,384]{2,1,0:T(8,128)(2,1)S(1)}, u32[]{:S(2)}, u32[]{:S(2)}) async-start(bf16[32,32,384]{2,1,0:T(8,128)(2,1)} %bitcast.84), calls=%async_computation.2 | async-start | bytes 1572864 | tf_op jit(solution)/shard_map/all_to_all | solution.py:1068
  173.9 42.9 %all-to-all-start.3 = ((bf16[32,32,1408]{2,1,0:T(8,128)(2,1)}), bf16[32,32,1408]{2,1,0:T(8,128)(2,1)S(1)}, u32[]{:S(2)}, u32[]{:S(2)}) async-start(bf16[32,32,1408]{2,1,0:T(8,128)(2,1)} %bitcast.21), calls=%async_computation.3 | async-start | bytes 5767168 | tf_op jit(solution)/shard_map/all_to_all | solution.py:1068
  178.0 164.3 %reduce-scatter.2.cloned.1.call-start = ((), (), s32[]{:S(2)}) async-start(), calls=%async_computation.11 | async-start | bytes 7864320 | tf_op jit(solution)/shard_map/reduce_scatter | solution.py:1286
  178.0 19.9 %collective-permute-start.7 = (bf16[1024,384]{1,0:T(8,128)(2,1)}, bf16[1024,384]{1,0:T(8,128)(2,1)S(1)}, u32[]{:S(2)}, u32[]{:S(2)}) collective-permute-start(bf16[1024,384]{1,0:T(8,128)(2,1)} %bitcast.81), channel_id=1, source_target_pairs={{0,1},{1,2},{2,3},{3,0},{4,5},{5,6},{6,7},{7,4},{8,9},{9,10},{10,1... | collective-permute-start | bytes 2359304 | tf_op jit(solution)/shard_map/ppermute | solution.py:1108
  179.8 19.9 %collective-permute-start.6 = (bf16[1024,384]{1,0:T(8,128)(2,1)}, bf16[1024,384]{1,0:T(8,128)(2,1)S(1)}, u32[]{:S(2)}, u32[]{:S(2)}) collective-permute-start(bf16[1024,384]{1,0:T(8,128)(2,1)} %bitcast.82), channel_id=1, source_target_pairs={{0,3},{1,0},{2,1},{3,2},{4,7},{5,4},{6,5},{7,6},{8,11},{9,8},{10,9... | collective-permute-start | bytes 2359304 | tf_op jit(solution)/shard_map/ppermute | solution.py:1109
  198.0 11.4 %collective-permute-start.8 = (bf16[512,384]{1,0:T(8,128)(2,1)S(1)}, bf16[512,384]{1,0:T(8,128)(2,1)}, u32[]{:S(2)}, u32[]{:S(2)}) collective-permute-start(bf16[512,384]{1,0:T(8,128)(2,1)S(1)} %slice.34), channel_id=1, source_target_pairs={{0,1},{1,2},{2,3},{3,0},{4,5},{5,6},{6,7},{7,4},{8,9},{9,10},{10,1... | collective-permute-start | bytes 1179656 | tf_op jit(solution)/shard_map/ppermute | solution.py:1110
  250.4 43.5 %all-to-all-start.4 = ((bf16[32,32,1408]{2,1,0:T(8,128)(2,1)}), bf16[32,32,1408]{2,1,0:T(8,128)(2,1)S(1)}, u32[]{:S(2)}, u32[]{:S(2)}) async-start(bf16[32,32,1408]{2,1,0:T(8,128)(2,1)} %bitcast.75), calls=%async_computation.4 | async-start | bytes 5767168 | tf_op jit(solution)/shard_map/all_to_all | solution.py:1068
  295.5 46.7 %all-to-all-start.5 = ((bf16[32,32,1536]{2,1,0:T(8,128)(2,1)}), bf16[32,32,1536]{2,1,0:T(8,128)(2,1)S(1)}, u32[]{:S(2)}, u32[]{:S(2)}) async-start(bf16[32,32,1536]{2,1,0:T(8,128)(2,1)} %bitcast.55), calls=%async_computation.5 | async-start | bytes 6291456 | tf_op jit(solution)/shard_map/all_to_all | solution.py:1068
  303.0 14.5 %collective-permute-start.10 = (bf16[64,1408]{1,0:T(8,128)(2,1)}, bf16[64,1408]{1,0:T(8,128)(2,1)S(1)}, u32[]{:S(2)}, u32[]{:S(2)}) collective-permute-start(bf16[64,1408]{1,0:T(8,128)(2,1)} %get-tuple-element.152.refs_0_), channel_id=1, source_target_pairs={{0,1},{1,0},{2,3},{3,2},{4,5},{5,4},{6,7},{7,6},{8,9},{9,8},{10,11... | collective-permute-start | bytes 540680 | tf_op jit(solution)/shard_map/ppermute | solution.py:1089
  304.9 12.6 %collective-permute-start.11 = (bf16[64,1408]{1,0:T(8,128)(2,1)}, bf16[64,1408]{1,0:T(8,128)(2,1)S(1)}, u32[]{:S(2)}, u32[]{:S(2)}) collective-permute-start(bf16[64,1408]{1,0:T(8,128)(2,1)} %get-tuple-element.154.refs_2_), channel_id=1, source_target_pairs={{0,3},{1,2},{2,1},{3,0},{4,7},{5,6},{6,5},{7,4},{8,11},{9,10},{10,... | collective-permute-start | bytes 540680 | tf_op jit(solution)/shard_map/ppermute | solution.py:1090
  320.9 21.3 %collective-permute-start.12 = (bf16[64,1408]{1,0:T(8,128)(2,1)}, bf16[64,1408]{1,0:T(8,128)(2,1)S(1)}, u32[]{:S(2)}, u32[]{:S(2)}) collective-permute-start(bf16[64,1408]{1,0:T(8,128)(2,1)} %get-tuple-element.174.refs_4_), channel_id=1, source_target_pairs={{0,3},{1,2},{2,1},{3,0},{4,7},{5,6},{6,5},{7,4},{8,11},{9,10},{10,... | collective-permute-start | bytes 540680 | tf_op jit(solution)/shard_map/ppermute | solution.py:1092
  320.9 21.3 %collective-permute-start.13 = (bf16[64,1408]{1,0:T(8,128)(2,1)}, bf16[64,1408]{1,0:T(8,128)(2,1)S(1)}, u32[]{:S(2)}, u32[]{:S(2)}) collective-permute-start(bf16[64,1408]{1,0:T(8,128)(2,1)} %get-tuple-element.176.refs_6_), channel_id=1, source_target_pairs={{0,1},{1,0},{2,3},{3,2},{4,5},{5,4},{6,7},{7,6},{8,9},{9,8},{10,11... | collective-permute-start | bytes 540680 | tf_op jit(solution)/shard_map/ppermute | solution.py:1093
  347.2 41.7 %all-to-all-start.6 = ((bf16[32,32,768]{2,1,0:T(8,128)(2,1)}), bf16[32,32,768]{2,1,0:T(8,128)(2,1)S(1)}, u32[]{:S(2)}, u32[]{:S(2)}) async-start(bf16[32,32,768]{2,1,0:T(8,128)(2,1)} %bitcast.77), calls=%async_computation.7 | async-start | bytes 3145728 | tf_op jit(solution)/shard_map/all_to_all | solution.py:1068
  354.5 121.0 %all-gather.8.cloned.1.call-start = ((), (), s32[]{:S(2)}) async-start(), calls=%async_computation.12 | async-start | bytes 10813440 | tf_op jit(solution)/shard_map/all_gather | solution.py:1333
  390.6 35.8 %all-to-all-start.7 = ((bf16[32,192,128]{2,1,0:T(8,128)(2,1)}), bf16[32,192,128]{2,1,0:T(8,128)(2,1)S(1)}, u32[]{:S(2)}, u32[]{:S(2)}) async-start(bf16[32,192,128]{2,1,0:T(8,128)(2,1)} %pad_maximum_fusion), calls=%async_computation.8 | async-start | bytes 3145728 | tf_op jit(solution)/shard_map/all_to_all | solution.py:1068
  412.4 12.4 %collective-permute-start.19 = (bf16[48,768]{1,0:T(8,128)(2,1)S(1)}, bf16[48,768]{1,0:T(8,128)(2,1)S(1)}, u32[]{:S(2)}, u32[]{:S(2)}) collective-permute-start(bf16[48,768]{1,0:T(8,128)(2,1)S(1)} %add_convert_fusion.10), channel_id=1, source_target_pairs={{0,8},{4,12},{8,0},{12,4},{16,24},{20,28},{24,16},{28,20},{32,40},... | collective-permute-start | bytes 221192 | tf_op jit(solution)/shard_map/ppermute | solution.py:1132
  414.3 17.8 %collective-permute-start.28 = (bf16[64,2880]{1,0:T(8,128)(2,1)}, bf16[64,2880]{1,0:T(8,128)(2,1)S(1)}, u32[]{:S(2)}, u32[]{:S(2)}) collective-permute-start(bf16[64,2880]{1,0:T(8,128)(2,1)} %get-tuple-element.198), channel_id=1, source_target_pairs={{0,3},{1,2},{2,1},{3,0},{4,7},{5,6},{6,5},{7,4},{8,11},{9,10},{10,... | collective-permute-start | bytes 1105928 | tf_op jit(solution)/shard_map/ppermute | solution.py:1090
  427.0 16.6 %collective-permute-start.26 = (bf16[64,2880]{1,0:T(8,128)(2,1)}, bf16[64,2880]{1,0:T(8,128)(2,1)S(1)}, u32[]{:S(2)}, u32[]{:S(2)}) collective-permute-start(bf16[64,2880]{1,0:T(8,128)(2,1)} %get-tuple-element.197), channel_id=1, source_target_pairs={{0,1},{1,0},{2,3},{3,2},{4,5},{5,4},{6,7},{7,6},{8,9},{9,8},{10,11... | collective-permute-start | bytes 1105928 | tf_op jit(solution)/shard_map/ppermute | solution.py:1089
  433.3 32.7 %collective-permute-start.29 = (bf16[64,2880]{1,0:T(8,128)(2,1)S(1)}, bf16[64,2880]{1,0:T(8,128)(2,1)S(1)}, u32[]{:S(2)}, u32[]{:S(2)}) collective-permute-start(bf16[64,2880]{1,0:T(8,128)(2,1)S(1)} %add_convert_fusion.refs_2_), channel_id=1, source_target_pairs={{0,1},{1,0},{2,3},{3,2},{4,5},{5,4},{6,7},{7,6},{8,9},{9,8},{10,11... | collective-permute-start | bytes 1105928 | tf_op jit(solution)/shard_map/ppermute | solution.py:1093
  443.7 22.2 %collective-permute-start.27 = (bf16[64,2880]{1,0:T(8,128)(2,1)S(1)}, bf16[64,2880]{1,0:T(8,128)(2,1)S(1)}, u32[]{:S(2)}, u32[]{:S(2)}) collective-permute-start(bf16[64,2880]{1,0:T(8,128)(2,1)S(1)} %add_convert_fusion.1.refs_0_), channel_id=1, source_target_pairs={{0,3},{1,2},{2,1},{3,0},{4,7},{5,6},{6,5},{7,4},{8,11},{9,10},{10,... | collective-permute-start | bytes 1105928 | tf_op jit(solution)/shard_map/ppermute | solution.py:1092
  456.6 14.5 %collective-permute-start.23 = (bf16[128,768]{1,0:T(8,128)(2,1)}, bf16[128,768]{1,0:T(8,128)(2,1)S(1)}, u32[]{:S(2)}, u32[]{:S(2)}) collective-permute-start(bf16[128,768]{1,0:T(8,128)(2,1)} %mix_results.1.refs_0_), channel_id=1, source_target_pairs={{0,3},{1,0},{2,1},{3,2},{4,7},{5,4},{6,5},{7,6},{8,11},{9,8},{10,9... | collective-permute-start | bytes 589832 | tf_op jit(solution)/shard_map/ppermute | solution.py:1120
  457.4 13.7 %collective-permute-start.24 = (bf16[128,768]{1,0:T(8,128)(2,1)}, bf16[128,768]{1,0:T(8,128)(2,1)S(1)}, u32[]{:S(2)}, u32[]{:S(2)}) collective-permute-start(bf16[128,768]{1,0:T(8,128)(2,1)} %mix_results.1.refs_0_), channel_id=1, source_target_pairs={{0,2},{1,3},{2,0},{3,1},{4,6},{5,7},{6,4},{7,5},{8,10},{9,11},{10,... | collective-permute-start | bytes 589832 | tf_op jit(solution)/shard_map/ppermute | solution.py:1121
  458.9 12.2 %collective-permute-start.25 = (bf16[128,768]{1,0:T(8,128)(2,1)}, bf16[128,768]{1,0:T(8,128)(2,1)S(1)}, u32[]{:S(2)}, u32[]{:S(2)}) collective-permute-start(bf16[128,768]{1,0:T(8,128)(2,1)} %mix_results.1.refs_0_), channel_id=1, source_target_pairs={{0,1},{1,2},{2,3},{3,0},{4,5},{5,6},{6,7},{7,4},{8,9},{9,10},{10,1... | collective-permute-start | bytes 589832 | tf_op jit(solution)/shard_map/ppermute | solution.py:1119
  (68 other events, 502.1 us)
Sparse Core Ops, SparseCore 0:
  10.3 82.1 all-gather.3
  105.6 72.2 all-gather.5
  250.6 66.6 reduce-scatter.1
  389.0 72.8 all-gather.7
where the time goes:
time: 499 us; the launch traced here: 489 us
  Pallas kernels  181 us (36%)
  waiting for transfers between devices  153 us (31%)
  starting transfers between devices  95.9 us (19%)
  local copies, waits for them, and re-layouts  27.6 us (6%)
  other arithmetic  17.1 us (3%)
  between operations  15 us (3%)
    all_to_all x8, waiting for transfers between devices, exchange(): lax.all_to_all(rows.reshape(parts, count // parts, width), 'expert', spli...  69.9 us
    all_to_all x8, starting transfers between devices, exchange(): lax.all_to_all(rows.reshape(parts, count // parts, width), 'expert', spli...  44.9 us
    pallas_call x3, Pallas kernels, weight_grad(): pl.pallas_call(weight_grad_kernel, grid=(STEPS,), out_shape=out_shape, in...  29.7 us
    pallas_call x1, Pallas kernels, expert_step(): pl.pallas_call(functools.partial(expert_kernel, experts, len(near)), grid...  22.8 us
    ppermute x1, waiting for transfers between devices, on_device(): cotangent_before = lax.ppermute(cotangent_own, 'tensor', up)  20.1 us
    ppermute x1, waiting for transfers between devices, tensor_chunks(): before = lax.ppermute(own, 'tensor', up)  17.8 us
    ppermute x5, waiting for transfers between devices, expert_sum(): lax.ppermute(values, 'expert', [(i, i ^ mask) for i in range(count)])  16.7 us
    pallas_call x2, Pallas kernels, compact_product(): pl.pallas_call(functools.partial(compact_kernel, shard, shard_pad), grid=...  16.1 us
  transfers between devices with their start and end apart: 45, of which 22 were waited for; matrix products, arithmetic and copies ran while one was open for 6% of the time, Pallas kernels for 26%

commit v1 on v0

--- a/solution.py
+++ b/solution.py
@@ -135,8 +135,8 @@
         for side in range(2):
             head = 2 * pair + side
             mine = left if side == 0 else jnp.logical_not(left)
-            one = jnp.where(mine, query, 0.0).astype(LOW)
-            scores = dot(one, keys[group], NT) * HD ** (-0.5)
+            one = jnp.where(mine, query * HD ** (-0.5), 0.0).astype(LOW)
+            scores = dot(one, keys[group], NT)
             scores = jnp.where(allowed, scores, MASKED)
             sink = sink_ref[head]
             top = jnp.maximum(jnp.max(scores, axis=1, keepdims=True), sink)
@@ -144,7 +144,7 @@
             denom = jnp.sum(weights, axis=1, keepdims=True) + jnp.exp(sink - top)
             lse = top + jnp.log(denom)
             lse_all = jnp.where(lanes == head, lse, lse_all)
-            prob = (weights / denom).astype(LOW)
+            prob = (weights * (1.0 / denom)).astype(LOW)
             outs.append(dot(prob, values[group]))
         out_ref[:, cols] = jnp.where(left, outs[0], outs[1]).astype(LOW)
     lse_ref[...] = lse_all
@@ -584,12 +584,8 @@
 def gathered_kernel(shard, blocks_ref, rows_ref, *refs):
     *out_refs, sum_ref = refs
     blocks = blocks_ref.shape[0]
-    tokens = blocks_ref.shape[2]
-    total = None
-    for i in range(blocks):
-        rows = rows_ref[i * tokens : (i + 1) * tokens, :]
-        part = dot(blocks_ref[i], rows)
-        total = part if total is None else total + part
+    turned = jnp.concatenate([blocks_ref[i] for i in range(blocks)], axis=1)
+    total = dot(turned, rows_ref[...])
     first = pl.program_id(0) == 0
 
     @pl.when(first)

time: 499 us -> 499 us (level)
  no operation moved by 1% of the time
where the time goes in v1:
time: 499 us; the launch traced here: 489 us
  Pallas kernels  181 us (36%)
  waiting for transfers between devices  153 us (31%)
  starting transfers between devices  95.8 us (19%)
  local copies, waits for them, and re-layouts  27.6 us (6%)
  other arithmetic  17.1 us (3%)
  between operations  15 us (3%)
    all_to_all x8, waiting for transfers between devices, exchange(): lax.all_to_all(rows.reshape(parts, count // parts, width), 'expert', spli...  69.9 us
    all_to_all x8, starting transfers between devices, exchange(): lax.all_to_all(rows.reshape(parts, count // parts, width), 'expert', spli...  44.9 us
    pallas_call x3, Pallas kernels, weight_grad(): pl.pallas_call(weight_grad_kernel, grid=(STEPS,), out_shape=out_shape, in...  29.7 us
    pallas_call x1, Pallas kernels, expert_step(): pl.pallas_call(functools.partial(expert_kernel, experts, len(near)), grid...  22.8 us
    ppermute x1, waiting for transfers between devices, on_device(): cotangent_before = lax.ppermute(cotangent_own, 'tensor', up)  20.1 us
    ppermute x1, waiting for transfers between devices, tensor_chunks(): before = lax.ppermute(own, 'tensor', up)  17.8 us
    ppermute x5, waiting for transfers between devices, expert_sum(): lax.ppermute(values, 'expert', [(i, i ^ mask) for i in range(count)])  16.7 us
    pallas_call x2, Pallas kernels, compact_product(): pl.pallas_call(functools.partial(compact_kernel, shard, shard_pad), grid=...  16.1 us
  transfers between devices with their start and end apart: 45, of which 22 were waited for; matrix products, arithmetic and copies ran while one was open for 6% of the time, Pallas kernels for 26%

profile of v1, /device:TPU:32, one launch (start us, length us, event | category | flops | bytes accessed | tf_op | source)
XLA Modules:
  0.0 489.0 jit_solution(15241425510113755594)
XLA Ops:
  16.0 7.5 %all-to-all-start = ((bf16[32,32,768]{2,1,0:T(8,128)(2,1)}), bf16[32,32,768]{2,1,0:T(8,128)(2,1)S(1)}, u32[]{:S(2)}, u32[]{:S(2)}) async-start(bf16[32,32,768]{2,1,0:T(8,128)(2,1)} %bitcast.63), calls=%async_computation | async-start | bytes 3145728 | tf_op jit(solution)/shard_map/all_to_all | solution.py:1064
  23.9 28.8 %all-to-all-done = bf16[32,32,768]{2,1,0:T(8,128)(2,1)S(1)} async-done(((bf16[32,32,768]{2,1,0:T(8,128)(2,1)}), bf16[32,32,768]{2,1,0:T(8,128)(2,1)S(1)}, u32[]{:S(2)}, u32[]{:S(2)}) %all-to-all-start) | async-done | bytes 1572896 | tf_op jit(solution)/shard_map/all_to_all | solution.py:1064
  67.8 20.1 %collective-permute-done.refs_3_ = bf16[1024,768]{1,0:T(8,128)(2,1)} collective-permute-done((bf16[1024,768]{1,0:T(8,128)(2,1)S(1)}, bf16[1024,768]{1,0:T(8,128)(2,1)}, u32[]{:S(2)}, u32[]{:S(2)}) %collective-permute-start) | collective-permute-done | bytes 1572896 | tf_op jit(solution)/shard_map/ppermute | solution.py:1202
  92.5 13.0 %attend_forward.1 = (bf16[128,1024]{1,0:T(8,128)(2,1)}, bf16[128,1280]{1,0:T(8,128)(2,1)}, f32[128,128]{1,0:T(8,128)}) custom-call(f32[16]{0:T(128)} %sink_ref.3, bf16[128,3072]{1,0:T(8,128)(2,1)} %copy.88.rows_ref.refs_0_, bf16[3072,2304]{1,0:T(8,128)(2,1)} %all-gather.4.cloned.1.call-done.weights_ref, f32[1,1280]{1,0:T(1,128)} %broadcast_in_dim.34.bias_ref, ...), custom_call_target="tpu_custom_call" | custom-call | flops 1 | bytes 1 | tf_op jit(solution)/shard_map/attend_forward/pallas_call | solution.py:284
  105.5 6.4 %attn_output.1 = (bf16[64,2880]{1,0:T(8,128)(2,1)}, bf16[64,2880]{1,0:T(8,128)(2,1)}) custom-call(bf16[128,1024]{1,0:T(8,128)(2,1)} %get-tuple-element.121.left_ref, bf16[3072,2304]{1,0:T(8,128)(2,1)} %all-gather.4.cloned.1.call-done.weights_ref), custom_call_target="tpu_custom_call" | custom-call | flops 1 | bytes 1 | tf_op jit(solution)/shard_map/attn_output/pallas_call | solution.py:377
  115.3 5.5 %all-to-all-start.1 = ((bf16[32,32,768]{2,1,0:T(8,128)(2,1)}), bf16[32,32,768]{2,1,0:T(8,128)(2,1)S(1)}, u32[]{:S(2)}, u32[]{:S(2)}) async-start(bf16[32,32,768]{2,1,0:T(8,128)(2,1)} %bitcast.16), calls=%async_computation.1 | async-start | bytes 3145728 | tf_op jit(solution)/shard_map/all_to_all | solution.py:1064
  138.8 5.5 %token_forward.1 = (f32[128,2880]{1,0:T(8,128)}, f32[128,32]{1,0:T(8,128)}, bf16[128,2944]{1,0:T(8,128)(2,1)}, bf16[1024,384]{1,0:T(8,128)(2,1)}) custom-call(s32[1]{0:T(128)} %bitcast.place_ref, bf16[128,2880]{1,0:T(8,128)(2,1)} %copy.89.input_ref.refs_5_, bf16[64,2880]{1,0:T(8,128)(2,1)} %copy-done.14, bf16[64,2880]{1,0:T(8,128)(2,1)} %copy-done.25, ...), custom_call_target="tpu_custom_call" | custom-call | flops 1 | bytes 1 | tf_op jit(solution)/shard_map/token_forward/pallas_call | solution.py:434
  145.4 4.4 all-to-all-start.2
  152.1 4.3 place_rows.5
  156.4 10.5 %grad_hidden.1 = (f32[1024,768]{1,0:T(8,128)}, bf16[1024,2880]{1,0:T(8,128)(2,1)}) custom-call(s32[1]{0:T(128)} %bitcast.place_ref, bf16[1024,768]{1,0:T(8,128)(2,1)} %bitcast.66, bf16[1024,768]{1,0:T(8,128)(2,1)} %collective-permute-done.1.refs_1_, bf16[1024,768]{1,0:T(8,128)(2,1)} %bitcast.67, bf16[1024,768]{1,0:T(8,128)(2,1)} %collective-permute-done.refs_3_, ...), custom_call_target="tpu_custom_call" | custom-call | flops 1 | bytes 1 | tf_op jit(solution)/shard_map/grad_hidden/pallas_call | solution.py:828
  166.9 6.1 %all-to-all-done.2 = bf16[32,32,384]{2,1,0:T(8,128)(2,1)S(1)} async-done(((bf16[32,32,384]{2,1,0:T(8,128)(2,1)}), bf16[32,32,384]{2,1,0:T(8,128)(2,1)S(1)}, u32[]{:S(2)}, u32[]{:S(2)}) %all-to-all-start.2) | async-done | bytes 786464 | tf_op jit(solution)/shard_map/all_to_all | solution.py:1064
  173.9 4.1 all-to-all-start.3
  180.1 17.8 %collective-permute-done.7.refs_3_ = bf16[1024,384]{1,0:T(8,128)(2,1)S(1)} collective-permute-done((bf16[1024,384]{1,0:T(8,128)(2,1)}, bf16[1024,384]{1,0:T(8,128)(2,1)S(1)}, u32[]{:S(2)}, u32[]{:S(2)}) %collective-permute-start.7) | collective-permute-done | bytes 786464 | tf_op jit(solution)/shard_map/ppermute | solution.py:1104
  203.7 5.6 %collective-permute-done.8 = bf16[512,384]{1,0:T(8,128)(2,1)} collective-permute-done((bf16[512,384]{1,0:T(8,128)(2,1)S(1)}, bf16[512,384]{1,0:T(8,128)(2,1)}, u32[]{:S(2)}, u32[]{:S(2)}) %collective-permute-start.8) | collective-permute-done | bytes 393248 | tf_op jit(solution)/shard_map/ppermute | solution.py:1106
  218.4 22.8 %expert_step.1 = (bf16[1024,1408]{1,0:T(8,128)(2,1)}, bf16[1024,720]{1,0:T(8,128)(2,1)}, bf16[1024,768]{1,0:T(8,128)(2,1)}, bf16[1024,720]{1,0:T(8,128)(2,1)}, b...) custom-call(s32[1]{0:T(128)} %bitcast.place_ref, bf16[1024,384]{1,0:T(8,128)(2,1)} %bitcast.83, ...), custom_call_target="tpu_custom_call" | custom-call | flops 16986931200 | bytes 40734720 | tf_op jit(solution)/shard_map/expert_step/pallas_call | solution.py:958
  241.2 9.2 %expert_result.1 = bf16[4,1024,768]{2,1,0:T(8,128)(2,1)} custom-call(bf16[1024,720]{1,0:T(8,128)(2,1)} %get-tuple-element.165.act_ref, bf16[720,2880]{1,0:T(8,128)(2,1)} %bitcast.53, f32[1,2880]{1,0:T(1,128)} %broadcast_select_fusion.refs_5_.bias_ref), custom_call_target="tpu_custom_call" | custom-call | flops 1 | bytes 1 | tf_op jit(solution)/shard_map/expert_result/pallas_call | solution.py:860
  250.4 4.6 all-to-all-start.4
  255.0 9.3 %grad_rows.1 = bf16[1024,1536]{1,0:T(8,128)(2,1)} custom-call(bf16[1024,720]{1,0:T(8,128)(2,1)} %get-tuple-element.150.grad_gate_ref.left_ref, bf16[1024,720]{1,0:T(8,128)(2,1)} %get-tuple-element.160.grad_up_ref.left_ref, bf16[720,2880]{1,0:T(8,128)(2,1)} %bitcast.69, bf16[720,2880]{1,0:T(8,128)(2,1)} %bitcast.71), custom_call_target="tpu_custom_call" | custom-call | flops 1 | bytes 1 | tf_op jit(solution)/shard_map/grad_rows/pallas_call | solution.py:1009
  264.3 29.6 %all-to-all-done.4 = bf16[32,32,1408]{2,1,0:T(8,128)(2,1)S(1)} async-done(((bf16[32,32,1408]{2,1,0:T(8,128)(2,1)}), bf16[32,32,1408]{2,1,0:T(8,128)(2,1)S(1)}, u32[]{:S(2)}, u32[]{:S(2)}) %all-to-all-start.4) | async-done | bytes 2883616 | tf_op jit(solution)/shard_map/all_to_all | solution.py:1064
  295.5 4.1 all-to-all-start.5
  307.6 9.8 %weight_grad.3 = f32[720,2880]{1,0:T(8,128)} custom-call(bf16[1024,720]{1,0:T(8,128)(2,1)} %get-tuple-element.150.grad_gate_ref.left_ref, bf16[1024,2880]{1,0:T(8,128)(2,1)} %get-tuple-element.151.right_ref), custom_call_target="tpu_custom_call" | custom-call | flops 1 | bytes 1 | tf_op jit(solution)/shard_map/weight_grad/pallas_call | solution.py:1049
  322.3 9.8 %weight_grad.4 = f32[720,2880]{1,0:T(8,128)} custom-call(bf16[1024,720]{1,0:T(8,128)(2,1)} %get-tuple-element.160.grad_up_ref.left_ref, bf16[1024,2880]{1,0:T(8,128)(2,1)} %get-tuple-element.151.right_ref), custom_call_target="tpu_custom_call" | custom-call | flops 1 | bytes 1 | tf_op jit(solution)/shard_map/weight_grad/pallas_call | solution.py:1049
  332.1 10.1 %weight_grad.5 = (f32[720,2880]{1,0:T(8,128)}, f32[8,2880]{1,0:T(8,128)}) custom-call(bf16[1024,768]{1,0:T(8,128)(2,1)} %get-tuple-element.161.left_ref, bf16[1024,2880]{1,0:T(8,128)(2,1)} %get-tuple-element.162.right_ref), custom_call_target="tpu_custom_call" | custom-call | flops 1 | bytes 1 | tf_op jit(solution)/shard_map/weight_grad/pallas_call | solution.py:1049
  347.2 7.2 %all-to-all-start.6 = ((bf16[32,32,768]{2,1,0:T(8,128)(2,1)}), bf16[32,32,768]{2,1,0:T(8,128)(2,1)S(1)}, u32[]{:S(2)}, u32[]{:S(2)}) async-start(bf16[32,32,768]{2,1,0:T(8,128)(2,1)} %bitcast.77), calls=%async_computation.7 | async-start | bytes 3145728 | tf_op jit(solution)/shard_map/all_to_all | solution.py:1064
  371.2 6.8 %token_backward.1 = (f32[128,2880]{1,0:T(8,128)}, bf16[128,3072]{1,0:T(8,128)(2,1)}, bf16[32,96,128]{2,1,0:T(8,128)(2,1)}, bf16[32,768]{1,0:T(8,128)(2,1)}, f32[8,3072]{1,0:T(8,128)}) custom-call(s32[1]{0:T(128)} %bitcast.place_ref, bf16[64,1536]{1,0:T(8,128)(2,1)} %copy-done.16, bf16[64,1536]{1,0:T(8,128)(2,1)} %copy-done.28, bf16[64,1536]{1,0:T(8,128)(2,1)} %copy-done.15, ...), custom_call_target="tpu_custom_call" | custom-call | flops 1 | bytes 1 | tf_op jit(solution)/shard_map/token_backward/pallas_call | solution.py:645
  378.1 10.8 %attend_backward.1 = (bf16[128,1280]{1,0:T(8,128)(2,1)}, f32[1,128]{1,0:T(1,128)}) custom-call(f32[16]{0:T(128)} %sink_ref.3, bf16[128,3072]{1,0:T(8,128)(2,1)} %get-tuple-element.181.rows_ref, bf16[3072,2304]{1,0:T(8,128)(2,1)} %all-gather.4.cloned.1.call-done.weights_ref, bf16[128,1280]{1,0:T(8,128)(2,1)} %get-tuple-element.182.rot_ref, ...), custom_call_target="tpu_custom_call" | custom-call | flops 1 | bytes 1 | tf_op jit(solution)/shard_map/attend_backward/pallas_call | solution.py:318
  390.6 7.5 %all-to-all-start.7 = ((bf16[32,192,128]{2,1,0:T(8,128)(2,1)}), bf16[32,192,128]{2,1,0:T(8,128)(2,1)S(1)}, u32[]{:S(2)}, u32[]{:S(2)}) async-start(bf16[32,192,128]{2,1,0:T(8,128)(2,1)} %pad_maximum_fusion), calls=%async_computation.8 | async-start | bytes 3145728 | tf_op jit(solution)/shard_map/all_to_all | solution.py:1064
  398.6 9.7 %grad_normed.1 = (bf16[64,2880]{1,0:T(8,128)(2,1)}, bf16[64,2880]{1,0:T(8,128)(2,1)}, f32[1,2880]{1,0:T(1,128)}) custom-call(bf16[128,1280]{1,0:T(8,128)(2,1)} %get-tuple-element.186.left_ref, bf16[3072,2304]{1,0:T(8,128)(2,1)} %all-gather.4.cloned.1.call-done.weights_ref, bf16[128,3072]{1,0:T(8,128)(2,1)} %copy.88.rows_ref.refs_0_), custom_call_target="tpu_custom_call" | custom-call | flops 1 | bytes 1 | tf_op jit(solution)/shard_map/grad_normed/pallas_call | solution.py:377
  416.0 8.7 %collective-permute-done.19 = bf16[48,768]{1,0:T(8,128)(2,1)S(1)} collective-permute-done((bf16[48,768]{1,0:T(8,128)(2,1)S(1)}, bf16[48,768]{1,0:T(8,128)(2,1)S(1)}, u32[]{:S(2)}, u32[]{:S(2)}) %collective-permute-start.19) | collective-permute-done | bytes 73760 | tf_op jit(solution)/shard_map/ppermute | solution.py:1128
  435.3 6.0 %output_grad.1 = f32[90,1024]{1,0:T(8,128)} custom-call(bf16[32,192,128]{2,1,0:T(8,128)(2,1)} %copy-done, bf16[4096,1024]{1,0:T(8,128)(2,1)} %all-gather.6.cloned.1.call-done.rows_ref), custom_call_target="tpu_custom_call" | custom-call | flops 1 | bytes 1 | tf_op jit(solution)/shard_map/output_grad/pallas_call | solution.py:619
  466.6 4.3 input_grad.1
  475.2 6.8 %qkv_grad.1 = (f32[90,1024]{1,0:T(8,128)}, f32[90,128]{1,0:T(8,128)}, f32[90,128]{1,0:T(8,128)}, f32[1024]{0:T(1024)}, f32[128]{0:T(128)}, /*index=5*/f32[128]{0:T(128)}) custom-call(bf16[32,192,128]{2,1,0:T(8,128)(2,1)} %copy-done, bf16[4096,1280]{1,0:T(8,128)(2,1)} %all-gather.8.cloned.1.call-done.rows_ref), custom_call_target="tpu_custom_call" | custom-call | flops 1 | bytes 1 | tf_op jit(solution)/shard_map/qkv_grad/pallas_call | solution.py:619
  (257 shorter events, 157.5 us)
Async XLA Ops:
  7.2 85.3 %all-gather.4.cloned.1.call-start = ((), (), s32[]{:S(2)}) async-start(), calls=%async_computation.9 | async-start | bytes 14598144 | tf_op jit(solution)/shard_map/all_gather | solution.py:1178
  16.0 36.8 %all-to-all-start = ((bf16[32,32,768]{2,1,0:T(8,128)(2,1)}), bf16[32,32,768]{2,1,0:T(8,128)(2,1)S(1)}, u32[]{:S(2)}, u32[]{:S(2)}) async-start(bf16[32,32,768]{2,1,0:T(8,128)(2,1)} %bitcast.63), calls=%async_computation | async-start | bytes 3145728 | tf_op jit(solution)/shard_map/all_to_all | solution.py:1064
  23.5 193.3 %all-gather.6.cloned.1.call-start = ((), (), s32[]{:S(2)}) async-start(), calls=%async_computation.10 | async-start | bytes 8650752 | tf_op jit(solution)/shard_map/all_gather | solution.py:1243
  52.8 35.1 %collective-permute-start = (bf16[1024,768]{1,0:T(8,128)(2,1)S(1)}, bf16[1024,768]{1,0:T(8,128)(2,1)}, u32[]{:S(2)}, u32[]{:S(2)}) collective-permute-start(bf16[1024,768]{1,0:T(8,128)(2,1)S(1)} %bitcast.64), channel_id=1, source_target_pairs={{0,1},{1,2},{2,3},{3,0},{4,5},{5,6},{6,7},{7,4},{8,9},{9,10},{10,1... | collective-permute-start | bytes 4718600 | tf_op jit(solution)/shard_map/ppermute | solution.py:1202
  54.4 34.8 %collective-permute-start.1 = (bf16[1024,768]{1,0:T(8,128)(2,1)S(1)}, bf16[1024,768]{1,0:T(8,128)(2,1)}, u32[]{:S(2)}, u32[]{:S(2)}) collective-permute-start(bf16[1024,768]{1,0:T(8,128)(2,1)S(1)} %bitcast.65), channel_id=1, source_target_pairs={{0,3},{1,0},{2,1},{3,2},{4,7},{5,4},{6,5},{7,6},{8,11},{9,8},{10,9... | collective-permute-start | bytes 4718600 | tf_op jit(solution)/shard_map/ppermute | solution.py:1203
  111.9 11.2 %collective-permute-start.4 = (bf16[64,2880]{1,0:T(8,128)(2,1)}, bf16[64,2880]{1,0:T(8,128)(2,1)}, u32[]{:S(2)}, u32[]{:S(2)}) collective-permute-start(bf16[64,2880]{1,0:T(8,128)(2,1)} %get-tuple-element.123), channel_id=1, source_target_pairs={{0,3},{1,2},{2,1},{3,0},{4,7},{5,6},{6,5},{7,4},{8,11},{9,10},{10,... | collective-permute-start | bytes 1105928 | tf_op jit(solution)/shard_map/ppermute | solution.py:1086
  113.4 12.6 %collective-permute-start.2 = (bf16[64,2880]{1,0:T(8,128)(2,1)}, bf16[64,2880]{1,0:T(8,128)(2,1)}, u32[]{:S(2)}, u32[]{:S(2)}) collective-permute-start(bf16[64,2880]{1,0:T(8,128)(2,1)} %get-tuple-element.122), channel_id=1, source_target_pairs={{0,1},{1,0},{2,3},{3,2},{4,5},{5,4},{6,7},{7,6},{8,9},{9,8},{10,11... | collective-permute-start | bytes 1105928 | tf_op jit(solution)/shard_map/ppermute | solution.py:1085
  115.3 30.0 %all-to-all-start.1 = ((bf16[32,32,768]{2,1,0:T(8,128)(2,1)}), bf16[32,32,768]{2,1,0:T(8,128)(2,1)S(1)}, u32[]{:S(2)}, u32[]{:S(2)}) async-start(bf16[32,32,768]{2,1,0:T(8,128)(2,1)} %bitcast.16), calls=%async_computation.1 | async-start | bytes 3145728 | tf_op jit(solution)/shard_map/all_to_all | solution.py:1064
  127.1 11.0 %collective-permute-start.3 = (bf16[64,2880]{1,0:T(8,128)(2,1)S(1)}, bf16[64,2880]{1,0:T(8,128)(2,1)S(1)}, u32[]{:S(2)}, u32[]{:S(2)}) collective-permute-start(bf16[64,2880]{1,0:T(8,128)(2,1)S(1)} %add_convert_fusion.3.refs_0_), channel_id=1, source_target_pairs={{0,3},{1,2},{2,1},{3,0},{4,7},{5,6},{6,5},{7,4},{8,11},{9,10},{10,... | collective-permute-start | bytes 1105928 | tf_op jit(solution)/shard_map/ppermute | solution.py:1088
  145.4 27.6 %all-to-all-start.2 = ((bf16[32,32,384]{2,1,0:T(8,128)(2,1)}), bf16[32,32,384]{2,1,0:T(8,128)(2,1)S(1)}, u32[]{:S(2)}, u32[]{:S(2)}) async-start(bf16[32,32,384]{2,1,0:T(8,128)(2,1)} %bitcast.84), calls=%async_computation.2 | async-start | bytes 1572864 | tf_op jit(solution)/shard_map/all_to_all | solution.py:1064
  173.9 42.9 %all-to-all-start.3 = ((bf16[32,32,1408]{2,1,0:T(8,128)(2,1)}), bf16[32,32,1408]{2,1,0:T(8,128)(2,1)S(1)}, u32[]{:S(2)}, u32[]{:S(2)}) async-start(bf16[32,32,1408]{2,1,0:T(8,128)(2,1)} %bitcast.21), calls=%async_computation.3 | async-start | bytes 5767168 | tf_op jit(solution)/shard_map/all_to_all | solution.py:1064
  178.0 164.3 %reduce-scatter.2.cloned.1.call-start = ((), (), s32[]{:S(2)}) async-start(), calls=%async_computation.11 | async-start | bytes 7864320 | tf_op jit(solution)/shard_map/reduce_scatter | solution.py:1282
  178.0 19.9 %collective-permute-start.7 = (bf16[1024,384]{1,0:T(8,128)(2,1)}, bf16[1024,384]{1,0:T(8,128)(2,1)S(1)}, u32[]{:S(2)}, u32[]{:S(2)}) collective-permute-start(bf16[1024,384]{1,0:T(8,128)(2,1)} %bitcast.81), channel_id=1, source_target_pairs={{0,1},{1,2},{2,3},{3,0},{4,5},{5,6},{6,7},{7,4},{8,9},{9,10},{10,1... | collective-permute-start | bytes 2359304 | tf_op jit(solution)/shard_map/ppermute | solution.py:1104
  179.8 19.9 %collective-permute-start.6 = (bf16[1024,384]{1,0:T(8,128)(2,1)}, bf16[1024,384]{1,0:T(8,128)(2,1)S(1)}, u32[]{:S(2)}, u32[]{:S(2)}) collective-permute-start(bf16[1024,384]{1,0:T(8,128)(2,1)} %bitcast.82), channel_id=1, source_target_pairs={{0,3},{1,0},{2,1},{3,2},{4,7},{5,4},{6,5},{7,6},{8,11},{9,8},{10,9... | collective-permute-start | bytes 2359304 | tf_op jit(solution)/shard_map/ppermute | solution.py:1105
  197.9 11.4 %collective-permute-start.8 = (bf16[512,384]{1,0:T(8,128)(2,1)S(1)}, bf16[512,384]{1,0:T(8,128)(2,1)}, u32[]{:S(2)}, u32[]{:S(2)}) collective-permute-start(bf16[512,384]{1,0:T(8,128)(2,1)S(1)} %slice.34), channel_id=1, source_target_pairs={{0,1},{1,2},{2,3},{3,0},{4,5},{5,6},{6,7},{7,4},{8,9},{9,10},{10,1... | collective-permute-start | bytes 1179656 | tf_op jit(solution)/shard_map/ppermute | solution.py:1106
  250.4 43.5 %all-to-all-start.4 = ((bf16[32,32,1408]{2,1,0:T(8,128)(2,1)}), bf16[32,32,1408]{2,1,0:T(8,128)(2,1)S(1)}, u32[]{:S(2)}, u32[]{:S(2)}) async-start(bf16[32,32,1408]{2,1,0:T(8,128)(2,1)} %bitcast.75), calls=%async_computation.4 | async-start | bytes 5767168 | tf_op jit(solution)/shard_map/all_to_all | solution.py:1064
  295.5 46.7 %all-to-all-start.5 = ((bf16[32,32,1536]{2,1,0:T(8,128)(2,1)}), bf16[32,32,1536]{2,1,0:T(8,128)(2,1)S(1)}, u32[]{:S(2)}, u32[]{:S(2)}) async-start(bf16[32,32,1536]{2,1,0:T(8,128)(2,1)} %bitcast.55), calls=%async_computation.5 | async-start | bytes 6291456 | tf_op jit(solution)/shard_map/all_to_all | solution.py:1064
  302.9 14.5 %collective-permute-start.10 = (bf16[64,1408]{1,0:T(8,128)(2,1)}, bf16[64,1408]{1,0:T(8,128)(2,1)S(1)}, u32[]{:S(2)}, u32[]{:S(2)}) collective-permute-start(bf16[64,1408]{1,0:T(8,128)(2,1)} %get-tuple-element.152.refs_0_), channel_id=1, source_target_pairs={{0,1},{1,0},{2,3},{3,2},{4,5},{5,4},{6,7},{7,6},{8,9},{9,8},{10,11... | collective-permute-start | bytes 540680 | tf_op jit(solution)/shard_map/ppermute | solution.py:1085
  304.8 12.6 %collective-permute-start.11 = (bf16[64,1408]{1,0:T(8,128)(2,1)}, bf16[64,1408]{1,0:T(8,128)(2,1)S(1)}, u32[]{:S(2)}, u32[]{:S(2)}) collective-permute-start(bf16[64,1408]{1,0:T(8,128)(2,1)} %get-tuple-element.154.refs_2_), channel_id=1, source_target_pairs={{0,3},{1,2},{2,1},{3,0},{4,7},{5,6},{6,5},{7,4},{8,11},{9,10},{10,... | collective-permute-start | bytes 540680 | tf_op jit(solution)/shard_map/ppermute | solution.py:1086
  320.8 21.3 %collective-permute-start.12 = (bf16[64,1408]{1,0:T(8,128)(2,1)}, bf16[64,1408]{1,0:T(8,128)(2,1)S(1)}, u32[]{:S(2)}, u32[]{:S(2)}) collective-permute-start(bf16[64,1408]{1,0:T(8,128)(2,1)} %get-tuple-element.174.refs_4_), channel_id=1, source_target_pairs={{0,3},{1,2},{2,1},{3,0},{4,7},{5,6},{6,5},{7,4},{8,11},{9,10},{10,... | collective-permute-start | bytes 540680 | tf_op jit(solution)/shard_map/ppermute | solution.py:1088
  320.9 21.3 %collective-permute-start.13 = (bf16[64,1408]{1,0:T(8,128)(2,1)}, bf16[64,1408]{1,0:T(8,128)(2,1)S(1)}, u32[]{:S(2)}, u32[]{:S(2)}) collective-permute-start(bf16[64,1408]{1,0:T(8,128)(2,1)} %get-tuple-element.176.refs_6_), channel_id=1, source_target_pairs={{0,1},{1,0},{2,3},{3,2},{4,5},{5,4},{6,7},{7,6},{8,9},{9,8},{10,11... | collective-permute-start | bytes 540680 | tf_op jit(solution)/shard_map/ppermute | solution.py:1089
  347.2 41.7 %all-to-all-start.6 = ((bf16[32,32,768]{2,1,0:T(8,128)(2,1)}), bf16[32,32,768]{2,1,0:T(8,128)(2,1)S(1)}, u32[]{:S(2)}, u32[]{:S(2)}) async-start(bf16[32,32,768]{2,1,0:T(8,128)(2,1)} %bitcast.77), calls=%async_computation.7 | async-start | bytes 3145728 | tf_op jit(solution)/shard_map/all_to_all | solution.py:1064
  354.4 120.8 %all-gather.8.cloned.1.call-start = ((), (), s32[]{:S(2)}) async-start(), calls=%async_computation.12 | async-start | bytes 10813440 | tf_op jit(solution)/shard_map/all_gather | solution.py:1329
  390.6 35.8 %all-to-all-start.7 = ((bf16[32,192,128]{2,1,0:T(8,128)(2,1)}), bf16[32,192,128]{2,1,0:T(8,128)(2,1)S(1)}, u32[]{:S(2)}, u32[]{:S(2)}) async-start(bf16[32,192,128]{2,1,0:T(8,128)(2,1)} %pad_maximum_fusion), calls=%async_computation.8 | async-start | bytes 3145728 | tf_op jit(solution)/shard_map/all_to_all | solution.py:1064
  412.3 12.4 %collective-permute-start.19 = (bf16[48,768]{1,0:T(8,128)(2,1)S(1)}, bf16[48,768]{1,0:T(8,128)(2,1)S(1)}, u32[]{:S(2)}, u32[]{:S(2)}) collective-permute-start(bf16[48,768]{1,0:T(8,128)(2,1)S(1)} %add_convert_fusion.10), channel_id=1, source_target_pairs={{0,8},{4,12},{8,0},{12,4},{16,24},{20,28},{24,16},{28,20},{32,40},... | collective-permute-start | bytes 221192 | tf_op jit(solution)/shard_map/ppermute | solution.py:1128
  414.3 17.8 %collective-permute-start.28 = (bf16[64,2880]{1,0:T(8,128)(2,1)}, bf16[64,2880]{1,0:T(8,128)(2,1)S(1)}, u32[]{:S(2)}, u32[]{:S(2)}) collective-permute-start(bf16[64,2880]{1,0:T(8,128)(2,1)} %get-tuple-element.198), channel_id=1, source_target_pairs={{0,3},{1,2},{2,1},{3,0},{4,7},{5,6},{6,5},{7,4},{8,11},{9,10},{10,... | collective-permute-start | bytes 1105928 | tf_op jit(solution)/shard_map/ppermute | solution.py:1086
  427.0 16.4 %collective-permute-start.26 = (bf16[64,2880]{1,0:T(8,128)(2,1)}, bf16[64,2880]{1,0:T(8,128)(2,1)S(1)}, u32[]{:S(2)}, u32[]{:S(2)}) collective-permute-start(bf16[64,2880]{1,0:T(8,128)(2,1)} %get-tuple-element.197), channel_id=1, source_target_pairs={{0,1},{1,0},{2,3},{3,2},{4,5},{5,4},{6,7},{7,6},{8,9},{9,8},{10,11... | collective-permute-start | bytes 1105928 | tf_op jit(solution)/shard_map/ppermute | solution.py:1085
  433.2 32.5 %collective-permute-start.29 = (bf16[64,2880]{1,0:T(8,128)(2,1)S(1)}, bf16[64,2880]{1,0:T(8,128)(2,1)S(1)}, u32[]{:S(2)}, u32[]{:S(2)}) collective-permute-start(bf16[64,2880]{1,0:T(8,128)(2,1)S(1)} %add_convert_fusion.refs_2_), channel_id=1, source_target_pairs={{0,1},{1,0},{2,3},{3,2},{4,5},{5,4},{6,7},{7,6},{8,9},{9,8},{10,11... | collective-permute-start | bytes 1105928 | tf_op jit(solution)/shard_map/ppermute | solution.py:1089
  443.5 22.2 %collective-permute-start.27 = (bf16[64,2880]{1,0:T(8,128)(2,1)S(1)}, bf16[64,2880]{1,0:T(8,128)(2,1)S(1)}, u32[]{:S(2)}, u32[]{:S(2)}) collective-permute-start(bf16[64,2880]{1,0:T(8,128)(2,1)S(1)} %add_convert_fusion.1.refs_0_), channel_id=1, source_target_pairs={{0,3},{1,2},{2,1},{3,0},{4,7},{5,6},{6,5},{7,4},{8,11},{9,10},{10,... | collective-permute-start | bytes 1105928 | tf_op jit(solution)/shard_map/ppermute | solution.py:1088
  456.5 14.4 %collective-permute-start.23 = (bf16[128,768]{1,0:T(8,128)(2,1)}, bf16[128,768]{1,0:T(8,128)(2,1)S(1)}, u32[]{:S(2)}, u32[]{:S(2)}) collective-permute-start(bf16[128,768]{1,0:T(8,128)(2,1)} %mix_results.1.refs_0_), channel_id=1, source_target_pairs={{0,3},{1,0},{2,1},{3,2},{4,7},{5,4},{6,5},{7,6},{8,11},{9,8},{10,9... | collective-permute-start | bytes 589832 | tf_op jit(solution)/shard_map/ppermute | solution.py:1116
  457.2 13.7 %collective-permute-start.24 = (bf16[128,768]{1,0:T(8,128)(2,1)}, bf16[128,768]{1,0:T(8,128)(2,1)S(1)}, u32[]{:S(2)}, u32[]{:S(2)}) collective-permute-start(bf16[128,768]{1,0:T(8,128)(2,1)} %mix_results.1.refs_0_), channel_id=1, source_target_pairs={{0,2},{1,3},{2,0},{3,1},{4,6},{5,7},{6,4},{7,5},{8,10},{9,11},{10,... | collective-permute-start | bytes 589832 | tf_op jit(solution)/shard_map/ppermute | solution.py:1117
  458.7 12.2 %collective-permute-start.25 = (bf16[128,768]{1,0:T(8,128)(2,1)}, bf16[128,768]{1,0:T(8,128)(2,1)S(1)}, u32[]{:S(2)}, u32[]{:S(2)}) collective-permute-start(bf16[128,768]{1,0:T(8,128)(2,1)} %mix_results.1.refs_0_), channel_id=1, source_target_pairs={{0,1},{1,2},{2,3},{3,0},{4,5},{5,6},{6,7},{7,4},{8,9},{9,10},{10,1... | collective-permute-start | bytes 589832 | tf_op jit(solution)/shard_map/ppermute | solution.py:1115
  (68 other events, 501.4 us)
Sparse Core Ops, SparseCore 0:
  10.3 82.1 all-gather.3
  105.6 72.2 all-gather.5
  250.5 66.6 reduce-scatter.1
  389.0 72.8 all-gather.7
